TPU v7x, 32 devices: a whole 2x2x4 slice. The times are simulated.
32 devices in a mesh: gx: 8 (over y, x, core), gy: 4 (over z).
Axes of the slice: x: 2, y: 2, z: 4, core: 2. Of those that a mesh axis runs over, the one named last changes fastest.
Arguments:
- fields: float32 [4, 4, 320, 10240], P(None, None, 'gy', 'gx'), may hold values from -6 to 6
- owner: int32 [2048, 1], P(('gx', 'gy')), may hold values from 0 to 31; in each aligned block of 64 rows (0 to 63, 64 to 127, ...) at most 4 rows name the same one
Outputs:
- received: float32 [4096, 640], P(('gx', 'gy'))
Inputs may be any that keep to these rules, and one draw needn't show every extreme that they name: Among the blocks of one device, no owner is named more than 4 times, a bound that some block reaches.
All inputs are finite; a program needn't handle non-finite values.
Results may differ from a plain program's by a relative error of at most 0.0001.
Values sent between devices are 32-bit elements; how exact they have to be, the bound alone decides.
No kernel may reach another device: no remote copies, remote signals or barrier semaphores. Data moves between devices by JAX's collectives and lax.ppermute only.
A program may use at most 256 MiB of HBM per device.

v0:
```python
import functools

import jax
import jax.numpy as jnp
import numpy as np
from jax import lax
from jax.experimental import pallas as pl
from jax.experimental.pallas import tpu as pltpu
from jax.sharding import PartitionSpec as P

BLK = 4
RATIO = 10
LANES = 128
HIGHEST = lax.Precision.HIGHEST
SIGMA_CELLS = 2.8867513
PRODUCT_PAIRS = ((0, 0), (0, 1), (0, 2), (0, 3), (1, 1), (1, 2), (1, 3), (2, 2), (2, 3), (3, 3))
COMPONENTS = 4
TERMS = COMPONENTS + len(PRODUCT_PAIRS)
LEVELS = 4
ROWS = 8
VMEM_BYTES = 24 * 1024 * 1024


def gauss_taps():
    spread = np.arange(21, dtype=np.float64) - 10.0
    values = np.exp(-spread * spread / (2.0 * SIGMA_CELLS * SIGMA_CELLS))
    return (values / values.sum()).astype(np.float32)


TAPS = gauss_taps()
G = [float(v) for v in TAPS]


def east_weights(columns):
    fine = np.arange(columns)[:, None]
    coarse = np.arange(columns // RATIO)[None, :]
    tap = fine - RATIO * coarse + 5
    inside = (tap >= 0) & (tap <= 20)
    return np.where(inside, TAPS[np.clip(tap, 0, 20)], np.float32(0))


def beyond_weights():
    weights = np.zeros((2, 8, LANES), np.float32)
    weights[0, 0, :6] = TAPS[15:21]
    weights[1, 0, LANES - 5 :] = TAPS[0:5]
    return weights


def edge_places():
    places = np.zeros((16, LANES), np.float32)
    places[0, LANES - 1] = 1.0
    places[8, 0] = 1.0
    return places


def north_tile(field, level, store):
    def loads(p):
        return [field[c * LEVELS + level, pl.ds(p, ROWS, stride=RATIO), :] for c in range(COMPONENTS)]

    def weighed(values, weight, sums):
        scaled = [v * weight for v in values]
        terms = scaled + [scaled[a] * values[b] for a, b in PRODUCT_PAIRS]
        return terms if sums is None else [s + t for s, t in zip(sums, terms)]

    own = below = above = None
    for p in range(RATIO):
        values = loads(p)
        own = weighed(values, G[p + 5], own)
        if p <= 5:
            below = weighed(values, G[p + 15], below)
        if p >= 5:
            above = weighed(values, G[p - 5], above)
    row = lax.broadcasted_iota(jnp.int32, (ROWS, LANES), 0)
    for q in range(TERMS):
        from_next = jnp.where(row < ROWS - 1, pltpu.roll(below[q], ROWS - 1, 0), 0.0)
        from_last = jnp.where(row > 0, pltpu.roll(above[q], 1, 0), 0.0)
        store(q * LEVELS + level, own[q] + from_next + from_last, below[q][0:1, :], above[q][ROWS - 1 : ROWS, :])


def store_in(inner, edge, lead):
    def store(place, inside, before, after):
        inner[lead, pl.ds(place * ROWS, ROWS), :] = inside
        edge[lead, pl.ds(place, 1), :] = before
        edge[lead, pl.ds(TERMS * LEVELS + place, 1), :] = after

    return store


def side_kernel(fields, weights, inner, edge, message, tile, sems):
    last = fields.shape[-1] - LANES
    copies = [
        pltpu.make_async_copy(fields.at[:, :, pl.ds(start, LANES)], tile.at[side], sems.at[side])
        for side, start in enumerate((0, last))
    ]
    for copy in copies:
        copy.start()
    for side, copy in enumerate(copies):
        copy.wait()
        for level in range(LEVELS):
            north_tile(tile.at[side], level, store_in(inner, edge, side))
        sums = jnp.concatenate([inner[side], edge[side]], axis=0)
        message[side] = lax.dot_general(
            weights[side], sums, (((1,), (1,)), ((), ())), precision=HIGHEST, preferred_element_type=jnp.float32
        )


def inner_kernel(fields, inner, edge, tile, sems):
    count = inner.shape[0]

    def copy(t):
        return pltpu.make_async_copy(
            fields.at[:, :, pl.ds(pl.multiple_of((t + 1) * LANES, LANES), LANES)], tile.at[t], sems.at[t]
        )

    for t in range(count):
        copy(t).start()

    def step(t, carry):
        copy(t).wait()
        for level in range(LEVELS):
            north_tile(tile.at[t], level, store_in(inner, edge, t))
        return carry

    lax.fori_loop(0, count, step, 0)


def east_sums(sides, inner, weights):
    count = inner.shape[0]
    tiles = [sides[0]] + [inner[t] for t in range(count)] + [sides[1]]
    total = None
    for t in range(0, count + 2, 2):
        pair = jnp.concatenate(tiles[t : t + 2], axis=1)
        part = jnp.dot(
            pair, weights[t * LANES : (t + 2) * LANES, :], precision=HIGHEST, preferred_element_type=jnp.float32
        )
        total = part if total is None else total + part
    return total


def from_sides(east, west, places):
    both = jnp.concatenate([east, west], axis=0)
    return lax.dot_general(
        both, places[...], (((0,), (0,)), ((), ())), precision=HIGHEST, preferred_element_type=jnp.float32
    )


def edge_kernel(sides, edge, weights, places, east, west, before, after):
    start = TERMS * LEVELS * ROWS
    total = east_sums(sides, edge, weights) + from_sides(east[:, start:], west[:, start:], places)
    half = TERMS * LEVELS
    before[...] = total[:half]
    after[...] = total[half:]


def coarse_kernel(sides, inner, weights, places, east, west, coarse):
    stop = TERMS * LEVELS * ROWS
    coarse[...] = east_sums(sides, inner, weights) + from_sides(east[:, :stop], west[:, :stop], places)


def send_kernel(cap, coarse, north, south, owner, outgoing, filtered, spread):
    filtered[...] = coarse[...]
    half = TERMS * LEVELS
    filtered[pl.ds(0, half, stride=ROWS), :] += south[...]
    filtered[pl.ds(ROWS - 1, half, stride=ROWS), :] += north[...]
    slab = LEVELS * ROWS
    means = [filtered[c * slab : (c + 1) * slab, :] for c in range(COMPONENTS)]
    lane = lax.broadcasted_iota(jnp.int32, (slab, LANES), 1) % BLK
    for k, (a, b) in enumerate(PRODUCT_PAIRS):
        q = COMPONENTS + k
        stress = filtered[q * slab : (q + 1) * slab, :] - means[a] * means[b]
        for c in range(BLK):
            spread[pl.ds(k * slab * BLK + c, slab, stride=BLK), :] = jnp.where(lane == c, stress, 0.0)
    slots = outgoing.shape[0] * outgoing.shape[1]
    blocks = owner.shape[0]
    across = LANES // BLK
    index = lax.broadcasted_iota(jnp.int32, (blocks, LANES), 0)
    named = jnp.broadcast_to(owner[...], (blocks, LANES))
    slot_row = lax.broadcasted_iota(jnp.int32, (slots, LANES), 0)
    stresses = spread[...].reshape(len(PRODUCT_PAIRS) * LEVELS, blocks // across, BLK * BLK, LANES)
    total = None
    for by in range(blocks // across):
        block = by * across + lax.broadcasted_iota(jnp.int32, (blocks, LANES), 1) // BLK
        mine = jnp.sum(jnp.where(index == block, named, 0), axis=0, keepdims=True)
        earlier = jnp.where((index < block) & (named == mine), 1, 0)
        slot = mine * cap + jnp.sum(earlier, axis=0, keepdims=True)
        chosen = jnp.where(slot_row == slot, 1.0, 0.0)
        payload = stresses[:, by].reshape(-1, LANES)
        part = lax.dot_general(
            chosen, payload, (((1,), (1,)), ((), ())), precision=HIGHEST, preferred_element_type=jnp.float32
        )
        total = part if total is None else total + part
    for d in range(outgoing.shape[0]):
        outgoing[d] = total[d * cap : (d + 1) * cap]


def call(kernel, out_shape, *args, scratch=(), hbm=0):
    whole = pl.BlockSpec(memory_space=pltpu.VMEM)
    return pl.pallas_call(
        kernel,
        out_shape=out_shape,
        in_specs=[pl.BlockSpec(memory_space=pl.ANY)] * hbm + [whole] * (len(args) - hbm),
        out_specs=jax.tree.map(lambda _: whole, out_shape),
        scratch_shapes=list(scratch),
        compiler_params=pltpu.CompilerParams(vmem_limit_bytes=VMEM_BYTES),
    )(*args)


def f32(*shape):
    return jax.ShapeDtypeStruct(shape, jnp.float32)


def per_device(fields, owner):
    _, _, height, width = fields.shape
    tiles = width // LANES
    places = TERMS * LEVELS
    rows = places * ROWS
    flat = fields.reshape(COMPONENTS * LEVELS, height, width)
    weights = jnp.asarray(east_weights(width))
    edge_at = jnp.asarray(edge_places())

    def tile_buffers(count):
        return [
            pltpu.VMEM((count, COMPONENTS * LEVELS, height, LANES), jnp.float32),
            pltpu.SemaphoreType.DMA((count,)),
        ]

    side_inner, side_edge, messages = call(
        side_kernel,
        (f32(2, rows, LANES), f32(2, 2 * places, LANES), f32(2, 8, rows + 2 * places)),
        flat,
        jnp.asarray(beyond_weights()),
        scratch=tile_buffers(2),
        hbm=1,
    )
    nx, ny = lax.axis_size("gx"), lax.axis_size("gy")
    up_x = [(i, (i + 1) % nx) for i in range(nx)]
    down_x = [(j, i) for i, j in up_x]
    up_y = [(i, (i + 1) % ny) for i in range(ny)]
    down_y = [(j, i) for i, j in up_y]
    from_east = lax.ppermute(messages[0], "gx", down_x)
    from_west = lax.ppermute(messages[1], "gx", up_x)
    inner, edge = call(
        inner_kernel,
        (f32(tiles - 2, rows, LANES), f32(tiles - 2, 2 * places, LANES)),
        flat,
        scratch=tile_buffers(tiles - 2),
        hbm=1,
    )
    before, after = call(
        edge_kernel, (f32(places, LANES), f32(places, LANES)), side_edge, edge, weights, edge_at, from_east, from_west
    )
    from_north = lax.ppermute(before, "gy", down_y)
    from_south = lax.ppermute(after, "gy", up_y)
    coarse = call(coarse_kernel, f32(rows, LANES), side_inner, inner, weights, edge_at, from_east, from_west)
    devices = nx * ny
    blocks = owner.shape[0]
    cap = max(2, 2 * blocks // devices)
    pay = len(PRODUCT_PAIRS) * LEVELS * BLK * BLK
    outgoing = call(
        functools.partial(send_kernel, cap),
        f32(devices, cap, pay),
        coarse,
        from_north,
        from_south,
        owner,
        scratch=[pltpu.VMEM((rows, LANES), jnp.float32), pltpu.VMEM((pay * blocks * BLK // LANES, LANES), jnp.float32)],
    )
    arrived = lax.all_to_all(outgoing, ("gx", "gy"), split_axis=0, concat_axis=0, tiled=True)
    return arrived.reshape(devices * cap, pay)


def solution(mesh):
    placed = (P(None, None, "gy", "gx"), P(("gx", "gy"), None))
    return jax.shard_map(
        per_device, mesh=mesh, in_specs=placed, out_specs=P(("gx", "gy"), None), check_vma=False
    )
```

profile of v0, /device:TPU:1, one launch (start us, length us, event | category | flops | bytes accessed | tf_op | source)
XLA Modules:
  0.0 37.8 jit_solution(8258194437117827572)
XLA Ops:
  0.0 0.0 copy-start
  0.0 2.9 %copy-done = f32[4,4,80,1280]{3,2,1,0:T(8,128)S(1)} copy-done((f32[4,4,80,1280]{3,2,1,0:T(8,128)S(1)}, f32[4,4,80,1280]{3,2,1,0:T(8,128)}, u32[]{:S(2)}) %copy-start) | copy-done | bytes 6553624
  2.9 0.0 copy-start.3
  2.9 0.7 %copy-done.3 = f32[2,8,128]{2,1,0:T(8,128)S(1)} copy-done((f32[2,8,128]{2,1,0:T(8,128)S(1)}, f32[2,8,128]{2,1,0:T(8,128)}, u32[]{:S(2)}) %copy-start.3) | copy-done | bytes 8216
  3.6 0.0 copy-start.1
  3.6 0.0 copy-start.2
  3.6 0.0 copy-start.4
  3.6 1.7 %shard_map.55 = (f32[2,448,128]{2,1,0:T(8,128)S(1)}, f32[2,112,128]{2,1,0:T(8,128)S(1)}, f32[2,8,560]{2,1,0:T(8,128)S(1)}) custom-call(f32[16,80,1280]{2,1,0:T(8,128)S(1)} %bitcast.5, f32[2,8,128]{2,1,0:T(8,128)S(1)} %copy-done.3), custom_call_target="tpu_custom_call" | custom-call | tf_op jit(solution)/shard_map/pallas_call | solution.py:198
  5.3 0.1 collective-permute-start
  5.4 2.6 %collective-permute-start.1 = (f32[8,560]{1,0:T(8,128)S(1)}, f32[8,560]{1,0:T(8,128)S(1)}, u32[]{:S(2)}, u32[]{:S(2)}) collective-permute-start(f32[8,560]{1,0:T(8,128)S(1)} %get-tuple-element.19), channel_id=1, source_target_pairs={{0,4},{4,8},{8,12},{12,16},{16,20},{20,24},{24,28},{28,0},{1,5},{5... | collective-permute-start | bytes 53768 | tf_op jit(solution)/shard_map/ppermute | solution.py:241
  8.0 3.8 %shard_map.56 = (f32[8,448,128]{2,1,0:T(8,128)S(1)}, f32[8,112,128]{2,1,0:T(8,128)S(1)}) custom-call(f32[16,80,1280]{2,1,0:T(8,128)S(1)} %bitcast.6), custom_call_target="tpu_custom_call" | custom-call | tf_op jit(solution)/shard_map/pallas_call | solution.py:198
  11.9 0.0 collective-permute-done.east
  11.9 0.0 collective-permute-done.1.west
  11.9 0.0 copy-done.1
  11.9 0.0 copy-done.2
  11.9 0.7 %shard_map.58 = (f32[56,128]{1,0:T(8,128)S(1)}, f32[56,128]{1,0:T(8,128)S(1)}) custom-call(f32[2,112,128]{2,1,0:T(8,128)S(1)} %get-tuple-element.15.sides, f32[8,112,128]{2,1,0:T(8,128)S(1)} %get-tuple-element.16.edge, f32[1280,128]{1,0:T(8,128)S(1)} %copy-done.1, f32[16,128]{1,0:T(8,128)S(1)} %copy-done.2, f32[8,560]{1,0:T(8,128)S(1)} %collective-permute-done.east, ...), custom_call_target="tpu_custom_call" | custom-call | tf_op jit(solution)/shard_map/pallas_call | solution.py:198
  12.6 3.4 %collective-permute-start.2 = (f32[56,128]{1,0:T(8,128)S(1)}, f32[56,128]{1,0:T(8,128)S(1)}, u32[]{:S(2)}, u32[]{:S(2)}) collective-permute-start(f32[56,128]{1,0:T(8,128)S(1)} %get-tuple-element.17), channel_id=1, source_target_pairs={{1,0},{2,1},{3,2},{0,3},{5,4},{6,5},{7,6},{4,7},{9,8},{10,9},{11,1... | collective-permute-start | bytes 86024 | tf_op jit(solution)/shard_map/ppermute | solution.py:252
  16.0 0.0 collective-permute-start.3
  16.0 0.0 copy-done.4
  16.0 0.1 copy.6.owner
  16.1 2.1 %shard_map.57.coarse = f32[448,128]{1,0:T(8,128)S(1)} custom-call(f32[2,448,128]{2,1,0:T(8,128)S(1)} %get-tuple-element.12.sides, f32[8,448,128]{2,1,0:T(8,128)S(1)} %get-tuple-element.13.inner, f32[1280,128]{1,0:T(8,128)S(1)} %copy-done.1, f32[16,128]{1,0:T(8,128)S(1)} %copy-done.2, f32[8,560]{1,0:T(8,128)S(1)} %collective-permute-done.east, ...), custom_call_target="tpu_custom_call" | custom-call | tf_op jit(solution)/shard_map/pallas_call | solution.py:198
  18.2 0.0 collective-permute-done.2.north
  18.2 2.3 %collective-permute-done.3.south = f32[56,128]{1,0:T(8,128)S(1)} collective-permute-done((f32[56,128]{1,0:T(8,128)S(1)}, f32[56,128]{1,0:T(8,128)S(1)}, u32[]{:S(2)}, u32[]{:S(2)}) %collective-permute-start.3) | collective-permute-done | bytes 28704 | tf_op jit(solution)/shard_map/ppermute | solution.py:253
  20.5 0.9 %shard_map.59 = f32[32,4,640]{2,1,0:T(4,128)S(1)} custom-call(f32[448,128]{1,0:T(8,128)S(1)} %shard_map.57.coarse, f32[56,128]{1,0:T(8,128)S(1)} %collective-permute-done.2.north, f32[56,128]{1,0:T(8,128)S(1)} %collective-permute-done.3.south, s32[64,1]{1,0:T(8,128)S(1)} %copy.6.owner), custom_call_target="tpu_custom_call" | custom-call | tf_op jit(solution)/shard_map/pallas_call | solution.py:198
  21.4 15.6 %all_to_all.5 = f32[32,4,640]{2,1,0:T(4,128)S(1)} all-to-all(f32[32,4,640]{2,1,0:T(4,128)S(1)} %shard_map.59), channel_id=1, replica_groups=mesh['gx'=8,'gy'=4] {'gx','gy'}, dimensions={0} | all-to-all | bytes 655360 | tf_op jit(solution)/shard_map/all_to_all | solution.py:268
  36.9 0.8 %reshape.7 = f32[128,640]{1,0:T(8,128)} reshape(f32[32,4,640]{2,1,0:T(4,128)S(1)} %all_to_all.5) | data formatting | bytes 655360 | tf_op jit(solution)/shard_map/reshape | solution.py:269
  (1 shorter events, 0.0 us)
Async XLA Ops:
  0.0 2.9 %copy-start = (f32[4,4,80,1280]{3,2,1,0:T(8,128)S(1)}, f32[4,4,80,1280]{3,2,1,0:T(8,128)}, u32[]{:S(2)}) copy-start(f32[4,4,80,1280]{3,2,1,0:T(8,128)} %param.5) | copy-start | bytes 19660804
  2.9 0.7 %copy-start.3 = (f32[2,8,128]{2,1,0:T(8,128)S(1)}, f32[2,8,128]{2,1,0:T(8,128)}, u32[]{:S(2)}) copy-start(f32[2,8,128]{2,1,0:T(8,128)} %constant.8.clone.weights) | copy-start | bytes 24580
  3.6 8.3 %copy-start.1 = (f32[1280,128]{1,0:T(8,128)S(1)}, f32[1280,128]{1,0:T(8,128)}, u32[]{:S(2)}) copy-start(f32[1280,128]{1,0:T(8,128)} %constant.6.clone.weights) | copy-start | bytes 1966084
  3.6 8.3 %copy-start.2 = (f32[16,128]{1,0:T(8,128)S(1)}, f32[16,128]{1,0:T(8,128)}, u32[]{:S(2)}) copy-start(f32[16,128]{1,0:T(8,128)} %constant.7.clone.places) | copy-start | bytes 24580
  3.6 12.4 %copy-start.4 = (s32[64,1]{0,1:T(1,128)S(1)}, s32[64,1]{0,1:T(1,128)}, u32[]{:S(2)}) copy-start(s32[64,1]{0,1:T(1,128)} %param.6) | copy-start | bytes 772
  5.3 6.6 %collective-permute-start = (f32[8,560]{1,0:T(8,128)S(1)}, f32[8,560]{1,0:T(8,128)S(1)}, u32[]{:S(2)}, u32[]{:S(2)}) collective-permute-start(f32[8,560]{1,0:T(8,128)S(1)} %get-tuple-element.20), channel_id=1, source_target_pairs={{4,0},{8,4},{12,8},{16,12},{20,16},{24,20},{28,24},{0,28},{5,1},{9... | collective-permute-start | bytes 53768 | tf_op jit(solution)/shard_map/ppermute | solution.py:240
  5.4 6.5 %collective-permute-start.1 = (f32[8,560]{1,0:T(8,128)S(1)}, f32[8,560]{1,0:T(8,128)S(1)}, u32[]{:S(2)}, u32[]{:S(2)}) collective-permute-start(f32[8,560]{1,0:T(8,128)S(1)} %get-tuple-element.19), channel_id=1, source_target_pairs={{0,4},{4,8},{8,12},{12,16},{16,20},{20,24},{24,28},{28,0},{1,5},{5... | collective-permute-start | bytes 53768 | tf_op jit(solution)/shard_map/ppermute | solution.py:241
  12.6 5.6 %collective-permute-start.2 = (f32[56,128]{1,0:T(8,128)S(1)}, f32[56,128]{1,0:T(8,128)S(1)}, u32[]{:S(2)}, u32[]{:S(2)}) collective-permute-start(f32[56,128]{1,0:T(8,128)S(1)} %get-tuple-element.17), channel_id=1, source_target_pairs={{1,0},{2,1},{3,2},{0,3},{5,4},{6,5},{7,6},{4,7},{9,8},{10,9},{11,1... | collective-permute-start | bytes 86024 | tf_op jit(solution)/shard_map/ppermute | solution.py:252
  16.0 4.5 %collective-permute-start.3 = (f32[56,128]{1,0:T(8,128)S(1)}, f32[56,128]{1,0:T(8,128)S(1)}, u32[]{:S(2)}, u32[]{:S(2)}) collective-permute-start(f32[56,128]{1,0:T(8,128)S(1)} %get-tuple-element.18), channel_id=1, source_target_pairs={{0,1},{1,2},{2,3},{3,0},{4,5},{5,6},{6,7},{7,4},{8,9},{9,10},{10,1... | collective-permute-start | bytes 86024 | tf_op jit(solution)/shard_map/ppermute | solution.py:253
where the time goes:
time: 38 us; the launch traced here: 37.8 us
  blocking collectives  15.6 us (41%)
  Pallas kernels  9.26 us (24%)
  starting transfers between devices  6.1 us (16%)
  local copies, waits for them, and re-layouts  4.5 us (12%)
  waiting for transfers between devices  2.27 us (6%)
    all_to_all x1, blocking collectives, per_device(): lax.all_to_all(outgoing, ('gx', 'gy'), split_axis=0, concat_axis=0, tiled...  15.6 us
    pallas_call x5, Pallas kernels, call(): pl.pallas_call(kernel, out_shape=out_shape, in_specs=[pl.BlockSpec(memory...  9.26 us
    unnamed x11, local copies, waits for them, and re-layouts  3.66 us
    ppermute x1, starting transfers between devices, per_device(): from_north = lax.ppermute(before, 'gy', down_y)  3.38 us
    ppermute x1, starting transfers between devices, per_device(): from_west = lax.ppermute(messages[1], 'gx', up_x)  2.61 us
    ppermute x1, waiting for transfers between devices, per_device(): from_south = lax.ppermute(after, 'gy', up_y)  2.26 us
    reshape x1, local copies, waits for them, and re-layouts, per_device(): return arrived.reshape(devices * cap, pay)  0.84 us
  transfers between devices with their start and end apart: 4, of which 1 were waited for; matrix products, arithmetic and copies ran while one was open for 0% of the time, Pallas kernels for 16%

commit v1 on v0

--- a/solution.py
+++ b/solution.py
@@ -18,6 +18,7 @@
 TERMS = COMPONENTS + len(PRODUCT_PAIRS)
 LEVELS = 4
 ROWS = 8
+EARLY = 4
 VMEM_BYTES = 24 * 1024 * 1024
 
 
@@ -39,10 +40,12 @@
     return np.where(inside, TAPS[np.clip(tap, 0, 20)], np.float32(0))
 
 
-def beyond_weights():
-    weights = np.zeros((2, 8, LANES), np.float32)
-    weights[0, 0, :6] = TAPS[15:21]
-    weights[1, 0, LANES - 5 :] = TAPS[0:5]
+def beyond_weights(side):
+    row = lax.broadcasted_iota(jnp.int32, (8, LANES), 0)
+    lane = lax.broadcasted_iota(jnp.int32, (8, LANES), 1)
+    weights = jnp.zeros((8, LANES), jnp.float32)
+    for at, tap in enumerate(G[15:21]) if side == 0 else enumerate(G[0:5], LANES - 5):
+        weights = jnp.where((row == 0) & (lane == at), tap, weights)
     return weights
 
 
@@ -86,53 +89,46 @@
     return store
 
 
-def side_kernel(fields, weights, inner, edge, message, tile, sems):
-    last = fields.shape[-1] - LANES
-    copies = [
-        pltpu.make_async_copy(fields.at[:, :, pl.ds(start, LANES)], tile.at[side], sems.at[side])
-        for side, start in enumerate((0, last))
+def tile_copies(fields, places, sems):
+    return [
+        pltpu.make_async_copy(fields.at[:, :, pl.ds(t * LANES, LANES)], place, sems.at[t]) for t, place in places
     ]
+
+
+def early_kernel(order, fields, inner, edge, message, later, tile, sems):
+    places = [(t, tile.at[i] if i < EARLY else later.at[i - EARLY]) for i, t in enumerate(order)]
+    copies = tile_copies(fields, places, sems)
     for copy in copies:
         copy.start()
-    for side, copy in enumerate(copies):
+    for i in range(EARLY):
+        copies[i].wait()
+        for level in range(LEVELS):
+            north_tile(tile.at[i], level, store_in(inner, edge, i))
+        if i < 2:
+            sums = jnp.concatenate([inner[i], edge[i]], axis=0)
+            message[i] = lax.dot_general(
+                beyond_weights(i), sums, (((1,), (1,)), ((), ())), precision=HIGHEST, preferred_element_type=jnp.float32
+            )
+    for copy in copies[EARLY:]:
         copy.wait()
-        for level in range(LEVELS):
-            north_tile(tile.at[side], level, store_in(inner, edge, side))
-        sums = jnp.concatenate([inner[side], edge[side]], axis=0)
-        message[side] = lax.dot_general(
-            weights[side], sums, (((1,), (1,)), ((), ())), precision=HIGHEST, preferred_element_type=jnp.float32
-        )
-
-
-def inner_kernel(fields, inner, edge, tile, sems):
-    count = inner.shape[0]
-
-    def copy(t):
-        return pltpu.make_async_copy(
-            fields.at[:, :, pl.ds(pl.multiple_of((t + 1) * LANES, LANES), LANES)], tile.at[t], sems.at[t]
-        )
-
-    for t in range(count):
-        copy(t).start()
-
+
+
+def later_kernel(tile, inner, edge):
     def step(t, carry):
-        copy(t).wait()
         for level in range(LEVELS):
             north_tile(tile.at[t], level, store_in(inner, edge, t))
         return carry
 
-    lax.fori_loop(0, count, step, 0)
-
-
-def east_sums(sides, inner, weights):
-    count = inner.shape[0]
-    tiles = [sides[0]] + [inner[t] for t in range(count)] + [sides[1]]
+    lax.fori_loop(0, tile.shape[0], step, 0)
+
+
+def east_sums(order, early, later, weights):
+    tiles = [early[t] for t in range(EARLY)] + [later[t] for t in range(len(order) - EARLY)]
     total = None
-    for t in range(0, count + 2, 2):
-        pair = jnp.concatenate(tiles[t : t + 2], axis=1)
-        part = jnp.dot(
-            pair, weights[t * LANES : (t + 2) * LANES, :], precision=HIGHEST, preferred_element_type=jnp.float32
-        )
+    for i in range(0, len(order), 2):
+        pair = jnp.concatenate(tiles[i : i + 2], axis=1)
+        rows = jnp.concatenate([weights[t * LANES : (t + 1) * LANES, :] for t in order[i : i + 2]], axis=0)
+        part = jnp.dot(pair, rows, precision=HIGHEST, preferred_element_type=jnp.float32)
         total = part if total is None else total + part
     return total
 
@@ -144,20 +140,20 @@
     )
 
 
-def edge_kernel(sides, edge, weights, places, east, west, before, after):
+def edge_kernel(order, early, later, weights, places, west, east, before, after):
     start = TERMS * LEVELS * ROWS
-    total = east_sums(sides, edge, weights) + from_sides(east[:, start:], west[:, start:], places)
+    total = east_sums(order, early, later, weights) + from_sides(east[:, start:], west[:, start:], places)
     half = TERMS * LEVELS
     before[...] = total[:half]
     after[...] = total[half:]
 
 
-def coarse_kernel(sides, inner, weights, places, east, west, coarse):
+def coarse_kernel(order, early, later, weights, places, west, east, coarse):
     stop = TERMS * LEVELS * ROWS
-    coarse[...] = east_sums(sides, inner, weights) + from_sides(east[:, :stop], west[:, :stop], places)
-
-
-def send_kernel(cap, coarse, north, south, owner, outgoing, filtered, spread):
+    coarse[...] = east_sums(order, early, later, weights) + from_sides(east[:, :stop], west[:, :stop], places)
+
+
+def send_kernel(cap, coarse, south, north, owner, outgoing, filtered, spread):
     filtered[...] = coarse[...]
     half = TERMS * LEVELS
     filtered[pl.ds(0, half, stride=ROWS), :] += south[...]
@@ -198,7 +194,7 @@
     return pl.pallas_call(
         kernel,
         out_shape=out_shape,
-        in_specs=[pl.BlockSpec(memory_space=pl.ANY)] * hbm + [whole] * (len(args) - hbm),
+        in_specs=[pl.BlockSpec(memory_space=pltpu.HBM)] * hbm + [whole] * (len(args) - hbm),
         out_specs=jax.tree.map(lambda _: whole, out_shape),
         scratch_shapes=list(scratch),
         compiler_params=pltpu.CompilerParams(vmem_limit_bytes=VMEM_BYTES),
@@ -218,18 +214,21 @@
     weights = jnp.asarray(east_weights(width))
     edge_at = jnp.asarray(edge_places())
 
-    def tile_buffers(count):
-        return [
-            pltpu.VMEM((count, COMPONENTS * LEVELS, height, LANES), jnp.float32),
-            pltpu.SemaphoreType.DMA((count,)),
-        ]
-
-    side_inner, side_edge, messages = call(
-        side_kernel,
-        (f32(2, rows, LANES), f32(2, 2 * places, LANES), f32(2, 8, rows + 2 * places)),
-        flat,
-        jnp.asarray(beyond_weights()),
-        scratch=tile_buffers(2),
+    order = (0, tiles - 1) + tuple(range(1, tiles - 1))
+    rest = tiles - EARLY
+    early_inner, early_edge, messages, later = call(
+        functools.partial(early_kernel, order),
+        (
+            f32(EARLY, rows, LANES),
+            f32(EARLY, 2 * places, LANES),
+            f32(2, 8, rows + 2 * places),
+            f32(rest, COMPONENTS * LEVELS, height, LANES),
+        ),
+        pltpu.with_memory_space_constraint(flat, pltpu.HBM),
+        scratch=[
+            pltpu.VMEM((EARLY, COMPONENTS * LEVELS, height, LANES), jnp.float32),
+            pltpu.SemaphoreType.DMA((tiles,)),
+        ],
         hbm=1,
     )
     nx, ny = lax.axis_size("gx"), lax.axis_size("gy")
@@ -237,21 +236,31 @@
     down_x = [(j, i) for i, j in up_x]
     up_y = [(i, (i + 1) % ny) for i in range(ny)]
     down_y = [(j, i) for i, j in up_y]
+    from_west = lax.ppermute(messages[1], "gx", up_x)
     from_east = lax.ppermute(messages[0], "gx", down_x)
-    from_west = lax.ppermute(messages[1], "gx", up_x)
-    inner, edge = call(
-        inner_kernel,
-        (f32(tiles - 2, rows, LANES), f32(tiles - 2, 2 * places, LANES)),
-        flat,
-        scratch=tile_buffers(tiles - 2),
-        hbm=1,
-    )
+    later_inner, later_edge = call(later_kernel, (f32(rest, rows, LANES), f32(rest, 2 * places, LANES)), later)
     before, after = call(
-        edge_kernel, (f32(places, LANES), f32(places, LANES)), side_edge, edge, weights, edge_at, from_east, from_west
-    )
+        functools.partial(edge_kernel, order),
+        (f32(places, LANES), f32(places, LANES)),
+        early_edge,
+        later_edge,
+        weights,
+        edge_at,
+        from_west,
+        from_east,
+    )
+    from_south = lax.ppermute(after, "gy", up_y)
     from_north = lax.ppermute(before, "gy", down_y)
-    from_south = lax.ppermute(after, "gy", up_y)
-    coarse = call(coarse_kernel, f32(rows, LANES), side_inner, inner, weights, edge_at, from_east, from_west)
+    coarse = call(
+        functools.partial(coarse_kernel, order),
+        f32(rows, LANES),
+        early_inner,
+        later_inner,
+        weights,
+        edge_at,
+        from_west,
+        from_east,
+    )
     devices = nx * ny
     blocks = owner.shape[0]
     cap = max(2, 2 * blocks // devices)
@@ -260,8 +269,8 @@
         functools.partial(send_kernel, cap),
         f32(devices, cap, pay),
         coarse,
+        from_south,
         from_north,
-        from_south,
         owner,
         scratch=[pltpu.VMEM((rows, LANES), jnp.float32), pltpu.VMEM((pay * blocks * BLK // LANES, LANES), jnp.float32)],
     )

time: 38 us -> 35.1 us (0.924)
  local copies, waits for them, and re-layouts: 4.5 us -> 0.95 us
  waiting for transfers between devices: 2.27 us -> 0.63 us
  blocking collectives: 15.6 us -> 17.2 us
  Pallas kernels: 9.26 us -> 9.98 us
    unnamed x11 -> x7, local copies, waits for them, and re-layouts: 3.66 us -> 0.11 us
    ppermute x1, waiting for transfers between devices: 2.26 us -> 0.01 us  [per_device(): from_south = lax.ppermute(after, 'gy', up_y)]
    all_to_all x1, blocking collectives: 15.6 us -> 17.2 us  [per_device(): lax.all_to_all(outgoing, ('gx', 'gy'), split_axis=0, concat_axis=0, tiled...]
    ppermute x1, starting transfers between devices: 0.01 us -> 1.35 us  [per_device(): from_south = lax.ppermute(after, 'gy', up_y)]
    ppermute x1, starting transfers between devices: 3.38 us -> 2.09 us  [per_device(): from_north = lax.ppermute(before, 'gy', down_y)]
    pallas_call x5, Pallas kernels: 9.26 us -> 9.98 us  [call(): pl.pallas_call(kernel, out_shape=out_shape, in_specs=[pl.BlockSpec(memory...]
    ppermute x1, waiting for transfers between devices: 0.01 us -> 0.63 us  [per_device(): from_east = lax.ppermute(messages[0], 'gx', down_x)]
  transfers between devices with their start and end apart: 4 -> 4, of which waited for: 1 -> 1; matrix products, arithmetic and copies ran while one was open for 0% -> 0% of each run, Pallas kernels for 16% -> 13%
where the time goes in v1:
time: 35.1 us; the launch traced here: 35 us
  blocking collectives  17.2 us (49%)
  Pallas kernels  9.98 us (28%)
  starting transfers between devices  6.1 us (17%)
  local copies, waits for them, and re-layouts  0.95 us (3%)
  waiting for transfers between devices  0.63 us (2%)
    all_to_all x1, blocking collectives, per_device(): lax.all_to_all(outgoing, ('gx', 'gy'), split_axis=0, concat_axis=0, tiled...  17.2 us
    pallas_call x5, Pallas kernels, call(): pl.pallas_call(kernel, out_shape=out_shape, in_specs=[pl.BlockSpec(memory...  9.98 us
    ppermute x1, starting transfers between devices, per_device(): from_west = lax.ppermute(messages[1], 'gx', up_x)  2.65 us
    ppermute x1, starting transfers between devices, per_device(): from_north = lax.ppermute(before, 'gy', down_y)  2.09 us
    ppermute x1, starting transfers between devices, per_device(): from_south = lax.ppermute(after, 'gy', up_y)  1.35 us
    reshape x1, local copies, waits for them, and re-layouts, per_device(): return arrived.reshape(devices * cap, pay)  0.84 us
  transfers between devices with their start and end apart: 4, of which 1 were waited for; matrix products, arithmetic and copies ran while one was open for 0% of the time, Pallas kernels for 13%

profile of v1, /device:TPU:1, one launch (start us, length us, event | category | flops | bytes accessed | tf_op | source)
XLA Modules:
  0.0 35.0 jit_solution(2615007602722963269)
XLA Ops:
  0.0 0.0 copy-start
  0.0 0.0 copy-start.1
  0.0 3.7 %shard_map.46 = (f32[4,448,128]{2,1,0:T(8,128)S(1)}, f32[4,112,128]{2,1,0:T(8,128)S(1)}, f32[2,8,560]{2,1,0:T(8,128)S(1)}, f32[6,16,80,128]{3,2,1,0:T(8,128)S(1)}) custom-call(f32[16,80,1280]{2,1,0:T(8,128)} %bitcast.5), custom_call_target="tpu_custom_call" | custom-call | tf_op jit(solution)/shard_map/pallas_call | solution.py:194
  3.7 0.0 copy-start.2
  3.7 2.7 %collective-permute-start = (f32[8,560]{1,0:T(8,128)S(1)}, f32[8,560]{1,0:T(8,128)S(1)}, u32[]{:S(2)}, u32[]{:S(2)}) collective-permute-start(f32[8,560]{1,0:T(8,128)S(1)} %get-tuple-element.22), channel_id=1, source_target_pairs={{0,4},{4,8},{8,12},{12,16},{16,20},{20,24},{24,28},{28,0},{1,5},{5... | collective-permute-start | bytes 53768 | tf_op jit(solution)/shard_map/ppermute | solution.py:239
  6.4 0.0 collective-permute-start.1
  6.4 2.6 %shard_map.47 = (f32[6,448,128]{2,1,0:T(8,128)S(1)}, f32[6,112,128]{2,1,0:T(8,128)S(1)}) custom-call(f32[6,16,80,128]{3,2,1,0:T(8,128)S(1)} %get-tuple-element.14.tile), custom_call_target="tpu_custom_call" | custom-call | tf_op jit(solution)/shard_map/pallas_call | solution.py:194
  9.0 0.0 collective-permute-done.west
  9.0 0.6 %collective-permute-done.1.east = f32[8,560]{1,0:T(8,128)S(1)} collective-permute-done((f32[8,560]{1,0:T(8,128)S(1)}, f32[8,560]{1,0:T(8,128)S(1)}, u32[]{:S(2)}, u32[]{:S(2)}) %collective-permute-start.1) | collective-permute-done | bytes 17952 | tf_op jit(solution)/shard_map/ppermute | solution.py:240
  9.6 0.0 copy-done
  9.6 0.0 copy-done.1
  9.6 0.7 %shard_map.49 = (f32[56,128]{1,0:T(8,128)S(1)}, f32[56,128]{1,0:T(8,128)S(1)}) custom-call(f32[4,112,128]{2,1,0:T(8,128)S(1)} %get-tuple-element.17.early, f32[6,112,128]{2,1,0:T(8,128)S(1)} %get-tuple-element.18.later, f32[1280,128]{1,0:T(8,128)S(1)} %copy-done, f32[16,128]{1,0:T(8,128)S(1)} %copy-done.1, f32[8,560]{1,0:T(8,128)S(1)} %collective-permute-done.west, ...), custom_call_target="tpu_custom_call" | custom-call | tf_op jit(solution)/shard_map/pallas_call | solution.py:194
  10.3 1.3 %collective-permute-start.2 = (f32[56,128]{1,0:T(8,128)S(1)}, f32[56,128]{1,0:T(8,128)S(1)}, u32[]{:S(2)}, u32[]{:S(2)}) collective-permute-start(f32[56,128]{1,0:T(8,128)S(1)} %get-tuple-element.19), channel_id=1, source_target_pairs={{0,1},{1,2},{2,3},{3,0},{4,5},{5,6},{6,7},{7,4},{8,9},{9,10},{10,1... | collective-permute-start | bytes 86024 | tf_op jit(solution)/shard_map/ppermute | solution.py:252
  11.6 2.1 %collective-permute-start.3 = (f32[56,128]{1,0:T(8,128)S(1)}, f32[56,128]{1,0:T(8,128)S(1)}, u32[]{:S(2)}, u32[]{:S(2)}) collective-permute-start(f32[56,128]{1,0:T(8,128)S(1)} %get-tuple-element.20), channel_id=1, source_target_pairs={{1,0},{2,1},{3,2},{0,3},{5,4},{6,5},{7,6},{4,7},{9,8},{10,9},{11,1... | collective-permute-start | bytes 86024 | tf_op jit(solution)/shard_map/ppermute | solution.py:253
  13.7 0.0 copy-done.2
  13.7 0.1 copy.5.owner
  13.8 2.1 %shard_map.48.coarse = f32[448,128]{1,0:T(8,128)S(1)} custom-call(f32[4,448,128]{2,1,0:T(8,128)S(1)} %get-tuple-element.13.early, f32[6,448,128]{2,1,0:T(8,128)S(1)} %get-tuple-element.15.later, f32[1280,128]{1,0:T(8,128)S(1)} %copy-done, f32[16,128]{1,0:T(8,128)S(1)} %copy-done.1, f32[8,560]{1,0:T(8,128)S(1)} %collective-permute-done.west, ...), custom_call_target="tpu_custom_call" | custom-call | tf_op jit(solution)/shard_map/pallas_call | solution.py:194
  16.0 0.0 collective-permute-done.2.south
  16.0 0.0 collective-permute-done.3.north
  16.0 0.9 %shard_map.50 = f32[32,4,640]{2,1,0:T(4,128)S(1)} custom-call(f32[448,128]{1,0:T(8,128)S(1)} %shard_map.48.coarse, f32[56,128]{1,0:T(8,128)S(1)} %collective-permute-done.2.south, f32[56,128]{1,0:T(8,128)S(1)} %collective-permute-done.3.north, s32[64,1]{1,0:T(8,128)S(1)} %copy.5.owner), custom_call_target="tpu_custom_call" | custom-call | tf_op jit(solution)/shard_map/pallas_call | solution.py:194
  16.9 17.2 %all_to_all.5 = f32[32,4,640]{2,1,0:T(4,128)S(1)} all-to-all(f32[32,4,640]{2,1,0:T(4,128)S(1)} %shard_map.50), channel_id=1, replica_groups=mesh['gx'=8,'gy'=4] {'gx','gy'}, dimensions={0} | all-to-all | bytes 655360 | tf_op jit(solution)/shard_map/all_to_all | solution.py:277
  34.1 0.8 %reshape.7 = f32[128,640]{1,0:T(8,128)} reshape(f32[32,4,640]{2,1,0:T(4,128)S(1)} %all_to_all.5) | data formatting | bytes 655360 | tf_op jit(solution)/shard_map/reshape | solution.py:278
  (1 shorter events, 0.0 us)
Async XLA Ops:
  0.0 9.6 %copy-start = (f32[1280,128]{1,0:T(8,128)S(1)}, f32[1280,128]{1,0:T(8,128)}, u32[]{:S(2)}) copy-start(f32[1280,128]{1,0:T(8,128)} %constant.4.clone.weights) | copy-start | bytes 1966084
  0.0 9.6 %copy-start.1 = (f32[16,128]{1,0:T(8,128)S(1)}, f32[16,128]{1,0:T(8,128)}, u32[]{:S(2)}) copy-start(f32[16,128]{1,0:T(8,128)} %constant.5.clone.places) | copy-start | bytes 24580
  3.7 10.0 %copy-start.2 = (s32[64,1]{0,1:T(1,128)S(1)}, s32[64,1]{0,1:T(1,128)}, u32[]{:S(2)}) copy-start(s32[64,1]{0,1:T(1,128)} %param.5) | copy-start | bytes 772
  3.7 5.2 %collective-permute-start = (f32[8,560]{1,0:T(8,128)S(1)}, f32[8,560]{1,0:T(8,128)S(1)}, u32[]{:S(2)}, u32[]{:S(2)}) collective-permute-start(f32[8,560]{1,0:T(8,128)S(1)} %get-tuple-element.22), channel_id=1, source_target_pairs={{0,4},{4,8},{8,12},{12,16},{16,20},{20,24},{24,28},{28,0},{1,5},{5... | collective-permute-start | bytes 53768 | tf_op jit(solution)/shard_map/ppermute | solution.py:239
  6.4 3.2 %collective-permute-start.1 = (f32[8,560]{1,0:T(8,128)S(1)}, f32[8,560]{1,0:T(8,128)S(1)}, u32[]{:S(2)}, u32[]{:S(2)}) collective-permute-start(f32[8,560]{1,0:T(8,128)S(1)} %get-tuple-element.21), channel_id=1, source_target_pairs={{4,0},{8,4},{12,8},{16,12},{20,16},{24,20},{28,24},{0,28},{5,1},{9... | collective-permute-start | bytes 53768 | tf_op jit(solution)/shard_map/ppermute | solution.py:240
  10.3 5.7 %collective-permute-start.2 = (f32[56,128]{1,0:T(8,128)S(1)}, f32[56,128]{1,0:T(8,128)S(1)}, u32[]{:S(2)}, u32[]{:S(2)}) collective-permute-start(f32[56,128]{1,0:T(8,128)S(1)} %get-tuple-element.19), channel_id=1, source_target_pairs={{0,1},{1,2},{2,3},{3,0},{4,5},{5,6},{6,7},{7,4},{8,9},{9,10},{10,1... | collective-permute-start | bytes 86024 | tf_op jit(solution)/shard_map/ppermute | solution.py:252
  11.6 4.3 %collective-permute-start.3 = (f32[56,128]{1,0:T(8,128)S(1)}, f32[56,128]{1,0:T(8,128)S(1)}, u32[]{:S(2)}, u32[]{:S(2)}) collective-permute-start(f32[56,128]{1,0:T(8,128)S(1)} %get-tuple-element.20), channel_id=1, source_target_pairs={{1,0},{2,1},{3,2},{0,3},{5,4},{6,5},{7,6},{4,7},{9,8},{10,9},{11,1... | collective-permute-start | bytes 86024 | tf_op jit(solution)/shard_map/ppermute | solution.py:253

commit v2 on v1

v2 whole, which is shorter than its diff:
```python
import functools

import jax
import jax.numpy as jnp
import numpy as np
from jax import lax
from jax.experimental import pallas as pl
from jax.experimental.pallas import tpu as pltpu
from jax.sharding import PartitionSpec as P

BLK = 4
RATIO = 10
LANES = 128
HIGHEST = lax.Precision.HIGHEST
SIGMA_CELLS = 2.8867513
PRODUCT_PAIRS = ((0, 0), (0, 1), (0, 2), (0, 3), (1, 1), (1, 2), (1, 3), (2, 2), (2, 3), (3, 3))
COMPONENTS = 4
TERMS = COMPONENTS + len(PRODUCT_PAIRS)
LEVELS = 4
ROWS = 8
OUTER = 2
READY = 3
PADDED = 16
EDGE = LEVELS * PADDED
VMEM_BYTES = 16 * 1024 * 1024


def gauss_taps():
    spread = np.arange(21, dtype=np.float64) - 10.0
    values = np.exp(-spread * spread / (2.0 * SIGMA_CELLS * SIGMA_CELLS))
    return (values / values.sum()).astype(np.float32)


TAPS = gauss_taps()
G = [float(v) for v in TAPS]


def east_weights(columns):
    fine = np.arange(columns)[:, None]
    coarse = np.arange(columns // RATIO)[None, :]
    tap = fine - RATIO * coarse + 5
    inside = (tap >= 0) & (tap <= 20)
    return np.where(inside, TAPS[np.clip(tap, 0, 20)], np.float32(0))


def beyond_weights(side):
    row = lax.broadcasted_iota(jnp.int32, (8, LANES), 0)
    lane = lax.broadcasted_iota(jnp.int32, (8, LANES), 1)
    weights = jnp.zeros((8, LANES), jnp.float32)
    for at, tap in enumerate(G[15:21]) if side == 0 else enumerate(G[0:5], LANES - 5):
        weights = jnp.where((row == 0) & (lane == at), tap, weights)
    return weights


def edge_places():
    odd = lax.axis_index("gx") % 2
    row = lax.broadcasted_iota(jnp.int32, (16, LANES), 0)
    lane = lax.broadcasted_iota(jnp.int32, (16, LANES), 1)
    across = odd * (LANES - 1)
    return jnp.where((row == 0) & (lane == across) | (row == 8) & (lane == LANES - 1 - across), 1.0, 0.0)


def weighed(values, weight, sums):
    scaled = [v * weight for v in values]
    terms = scaled + [scaled[a] * values[b] for a, b in PRODUCT_PAIRS]
    return terms if sums is None else [s + t for s, t in zip(sums, terms)]


def north_sums(load):
    own = below = above = None
    for p in range(RATIO):
        values = load(p)
        own = weighed(values, G[p + 5], own)
        if p <= 5:
            below = weighed(values, G[p + 15], below)
        if p >= 5:
            above = weighed(values, G[p - 5], above)
    row = lax.broadcasted_iota(jnp.int32, (ROWS, LANES), 0)
    inside = []
    for q in range(TERMS):
        from_next = jnp.where(row < ROWS - 1, pltpu.roll(below[q], ROWS - 1, 0), 0.0)
        from_last = jnp.where(row > 0, pltpu.roll(above[q], 1, 0), 0.0)
        inside.append(own[q] + from_next + from_last)
    return inside, below, above


def strided(tile, level, p):
    return [tile[c * LEVELS + level, pl.ds(p, ROWS, stride=RATIO), :] for c in range(COMPONENTS)]


def sublane_sums(values):
    row = lax.broadcasted_iota(jnp.int32, (ROWS, LANES), 0)

    def fours(a, b):
        return jnp.where(row < 4, a, b) + pltpu.roll(jnp.where(row < 4, b, a), 4, 0)

    def fewer(a, b, step):
        return jnp.where(row & step == 0, a + pltpu.roll(a, ROWS - step, 0), b + pltpu.roll(b, step, 0))

    u = [fours(values[i], values[i + 4]) for i in range(4)]
    return fewer(fewer(u[0], u[2], 2), fewer(u[1], u[3], 2), 1)


def end_taps(side):
    row = lax.broadcasted_iota(jnp.int32, (ROWS, LANES), 0)
    column = jnp.zeros((ROWS, LANES), jnp.float32)
    for r, tap in enumerate(G[15:21]) if side == 0 else enumerate(G[0:5], ROWS - 5):
        column = jnp.where(row == r, tap, column)
    return column


def end_sums(tile, edge):
    last = tile.shape[1] - ROWS
    for side, start in enumerate((0, last)):
        taps = end_taps(side)
        for level in range(LEVELS):
            values = [tile[c * LEVELS + level, pl.ds(start, ROWS), :] for c in range(COMPONENTS)]
            terms = weighed(values, taps, None)
            place = side * EDGE + level * PADDED
            edge[pl.ds(place, ROWS), :] = sublane_sums(terms[:ROWS])
            edge[pl.ds(place + ROWS, ROWS), :] = sublane_sums(terms[ROWS:] + terms[: 2 * ROWS - TERMS])


def filter_tile(tile, inner, edge=None):
    for level in range(LEVELS):
        inside, below, above = north_sums(functools.partial(strided, tile, level))
        for q in range(TERMS):
            inner[pl.ds((q * LEVELS + level) * ROWS, ROWS), :] = inside[q]
            if edge is not None:
                edge[pl.ds(level * PADDED + q, 1), :] = below[q][0:1]
                edge[pl.ds(EDGE + level * PADDED + q, 1), :] = above[q][ROWS - 1 : ROWS]


def clear_padding(edge):
    for level in range(2 * LEVELS):
        edge[pl.ds(level * PADDED + ROWS, ROWS), :] = jnp.zeros((ROWS, LANES), jnp.float32)


def tile_copies(fields, places, sems):
    return [
        pltpu.make_async_copy(fields.at[:, :, pl.ds(t * LANES, LANES)], place, sems.at[i])
        for i, (t, place) in enumerate(places)
    ]


def outer_kernel(order, fields, inner, edge, across, beside, ready, tile, sems):
    places = [(t, tile.at[i] if i < OUTER else ready.at[i - OUTER]) for i, t in enumerate(order[: OUTER + READY])]
    copies = tile_copies(fields, places, sems)
    for copy in copies:
        copy.start()
    messages = []
    for i in range(OUTER):
        clear_padding(edge.at[i])
        copies[i].wait()
        filter_tile(tile.at[i], inner.at[i], edge.at[i])
        sums = jnp.concatenate([inner[i], edge[i]], axis=0)
        messages.append(
            lax.dot_general(
                beyond_weights(i), sums, (((1,), (1,)), ((), ())), precision=HIGHEST, preferred_element_type=jnp.float32
            )
        )
    odd = lax.axis_index("gx") % 2 == 1
    across[...] = jnp.where(odd, messages[1], messages[0])
    beside[...] = jnp.where(odd, messages[0], messages[1])
    for copy in copies[OUTER:]:
        copy.wait()


def middle_kernel(order, fields, outer_edge, ready, weights, inner, partial, later, edge, sems):
    count = len(order) - OUTER - READY
    copies = tile_copies(fields, [(t, later.at[i]) for i, t in enumerate(order[OUTER + READY :])], sems)
    for copy in copies:
        copy.start()
    for i in range(READY):
        clear_padding(edge.at[i])
        filter_tile(ready.at[i], inner.at[i], edge.at[i])
    for i in range(count):
        copies[i].wait()
        end_sums(later.at[i], edge.at[READY + i])
    tiles = [outer_edge[i] for i in range(OUTER)] + [edge[i] for i in range(READY + count)]
    partial[...] = east_sums(order, tiles, weights)


def east_sums(order, tiles, weights):
    total = None
    for i in range(0, len(order), 2):
        pair = jnp.concatenate(tiles[i : i + 2], axis=1)
        rows = jnp.concatenate([weights[t * LANES : (t + 1) * LANES, :] for t in order[i : i + 2]], axis=0)
        part = jnp.dot(pair, rows, precision=HIGHEST, preferred_element_type=jnp.float32)
        total = part if total is None else total + part
    return total


def from_sides(across, beside):
    both = jnp.concatenate([across, beside], axis=0)
    return lax.dot_general(
        both, edge_places(), (((0,), (0,)), ((), ())), precision=HIGHEST, preferred_element_type=jnp.float32
    )


def corner_kernel(partial, across, beside, before, after):
    start = TERMS * LEVELS * ROWS
    total = partial[...] + from_sides(across[:, start:], beside[:, start:])
    before[...] = total[:EDGE]
    after[...] = total[EDGE:]


def coarse_kernel(order, outer_inner, ready_inner, later, weights, across, beside, coarse, inner):
    count = later.shape[0]
    for i in range(count):
        filter_tile(later.at[i], inner.at[i])
    tiles = [outer_inner[i] for i in range(OUTER)] + [ready_inner[i] for i in range(READY)]
    tiles += [inner[i] for i in range(count)]
    stop = TERMS * LEVELS * ROWS
    coarse[...] = east_sums(order, tiles, weights) + from_sides(across[:, :stop], beside[:, :stop])


def send_kernel(cap, coarse, south, north, owner, outgoing, filtered, spread):
    filtered[...] = coarse[...]
    slab = LEVELS * ROWS
    for level in range(LEVELS):
        filtered[pl.ds(level * ROWS, TERMS, stride=slab), :] += south[pl.ds(level * PADDED, TERMS), :]
        filtered[pl.ds(level * ROWS + ROWS - 1, TERMS, stride=slab), :] += north[pl.ds(level * PADDED, TERMS), :]
    means = [filtered[c * slab : (c + 1) * slab, :] for c in range(COMPONENTS)]
    lane = lax.broadcasted_iota(jnp.int32, (slab, LANES), 1) % BLK
    for k, (a, b) in enumerate(PRODUCT_PAIRS):
        q = COMPONENTS + k
        stress = filtered[q * slab : (q + 1) * slab, :] - means[a] * means[b]
        for c in range(BLK):
            spread[pl.ds(k * slab * BLK + c, slab, stride=BLK), :] = jnp.where(lane == c, stress, 0.0)
    slots = outgoing.shape[0] * outgoing.shape[1]
    blocks = owner.shape[1]
    across = LANES // BLK
    own = lax.broadcasted_iota(jnp.int32, (blocks, blocks), 0) == lax.broadcasted_iota(jnp.int32, (blocks, blocks), 1)
    column = jnp.sum(jnp.where(own, jnp.broadcast_to(owner[...], (blocks, blocks)), 0), axis=1, keepdims=True)
    index = lax.broadcasted_iota(jnp.int32, (blocks, LANES), 0)
    named = jnp.broadcast_to(column, (blocks, LANES))
    slot_row = lax.broadcasted_iota(jnp.int32, (slots, LANES), 0)
    stresses = spread[...].reshape(len(PRODUCT_PAIRS) * LEVELS, blocks // across, BLK * BLK, LANES)
    total = None
    for by in range(blocks // across):
        block = by * across + lax.broadcasted_iota(jnp.int32, (blocks, LANES), 1) // BLK
        mine = jnp.sum(jnp.where(index == block, named, 0), axis=0, keepdims=True)
        earlier = jnp.where((index < block) & (named == mine), 1, 0)
        slot = mine * cap + jnp.sum(earlier, axis=0, keepdims=True)
        chosen = jnp.where(slot_row == slot, 1.0, 0.0)
        payload = stresses[:, by].reshape(-1, LANES)
        part = lax.dot_general(
            chosen, payload, (((1,), (1,)), ((), ())), precision=HIGHEST, preferred_element_type=jnp.float32
        )
        total = part if total is None else total + part
    for d in range(outgoing.shape[0]):
        outgoing[d] = total[d * cap : (d + 1) * cap]


def call(kernel, out_shape, *args, scratch=(), hbm=0):
    whole = pl.BlockSpec(memory_space=pltpu.VMEM)
    held = [pltpu.with_memory_space_constraint(a, pltpu.VMEM if i >= hbm else pltpu.HBM) for i, a in enumerate(args)]
    return pl.pallas_call(
        kernel,
        out_shape=out_shape,
        in_specs=[pl.BlockSpec(memory_space=pltpu.HBM)] * hbm + [whole] * (len(args) - hbm),
        out_specs=jax.tree.map(lambda _: whole, out_shape),
        scratch_shapes=list(scratch),
        compiler_params=pltpu.CompilerParams(vmem_limit_bytes=VMEM_BYTES),
    )(*held)


def f32(*shape):
    return jax.ShapeDtypeStruct(shape, jnp.float32)


def per_device(fields, owner):
    _, _, height, width = fields.shape
    tiles = width // LANES
    rows = TERMS * LEVELS * ROWS
    fine = COMPONENTS * LEVELS
    flat = fields.reshape(fine, height, width)
    weights = jnp.asarray(east_weights(width))
    order = (0, tiles - 1) + tuple(range(1, tiles - 1))
    rest = tiles - OUTER - READY
    message = f32(8, rows + 2 * EDGE)
    outer_inner, outer_edge, to_across, to_beside, ready = call(
        functools.partial(outer_kernel, order),
        (
            f32(OUTER, rows, LANES),
            f32(OUTER, 2 * EDGE, LANES),
            message,
            message,
            f32(READY, fine, height, LANES),
        ),
        flat,
        scratch=[pltpu.VMEM((OUTER, fine, height, LANES), jnp.float32), pltpu.SemaphoreType.DMA((OUTER + READY,))],
        hbm=1,
    )
    nx, ny = lax.axis_size("gx"), lax.axis_size("gy")
    beside_x = [(i, i ^ 1) for i in range(nx)]
    across_x = [(i, (i + 1) % nx if i % 2 else (i - 1) % nx) for i in range(nx)]
    up_y = [(i, (i + 1) % ny) for i in range(ny)]
    down_y = [(j, i) for i, j in up_y]
    across = lax.ppermute(to_across, "gx", across_x)
    beside = lax.ppermute(to_beside, "gx", beside_x)
    ready_inner, partial, later = call(
        functools.partial(middle_kernel, order),
        (f32(READY, rows, LANES), f32(2 * EDGE, LANES), f32(rest, fine, height, LANES)),
        flat,
        outer_edge,
        ready,
        weights,
        scratch=[pltpu.VMEM((READY + rest, 2 * EDGE, LANES), jnp.float32), pltpu.SemaphoreType.DMA((rest,))],
        hbm=1,
    )
    before, after = call(corner_kernel, (f32(EDGE, LANES), f32(EDGE, LANES)), partial, across, beside)
    from_south = lax.ppermute(after, "gy", up_y)
    from_north = lax.ppermute(before, "gy", down_y)
    coarse = call(
        functools.partial(coarse_kernel, order),
        f32(rows, LANES),
        outer_inner,
        ready_inner,
        later,
        weights,
        across,
        beside,
        scratch=[pltpu.VMEM((rest, rows, LANES), jnp.float32)],
    )
    devices = nx * ny
    blocks = owner.shape[0]
    cap = max(2, 2 * blocks // devices)
    pay = len(PRODUCT_PAIRS) * LEVELS * BLK * BLK
    outgoing = call(
        functools.partial(send_kernel, cap),
        f32(devices, cap, pay),
        coarse,
        from_south,
        from_north,
        owner.reshape(1, blocks),
        scratch=[pltpu.VMEM((rows, LANES), jnp.float32), pltpu.VMEM((pay * blocks * BLK // LANES, LANES), jnp.float32)],
    )
    arrived = lax.all_to_all(outgoing, ("gx", "gy"), split_axis=0, concat_axis=0, tiled=True)
    return arrived.reshape(devices * cap, pay)


def solution(mesh):
    placed = (P(None, None, "gy", "gx"), P(("gx", "gy"), None))
    return jax.shard_map(
        per_device, mesh=mesh, in_specs=placed, out_specs=P(("gx", "gy"), None), check_vma=False
    )
```

time: 35.1 us -> 33.5 us (0.954)
  blocking collectives: 17.2 us -> 14.4 us
  Pallas kernels: 9.98 us -> 11.1 us
  starting transfers between devices: 6.1 us -> 6.89 us
  waiting for transfers between devices: 0.63 us -> 0.01 us
    all_to_all x1, blocking collectives: 17.2 us -> 14.4 us  [per_device(): lax.all_to_all(outgoing, ('gx', 'gy'), split_axis=0, concat_axis=0, tiled...]
    pallas_call x5, Pallas kernels: 9.98 us -> 11.1 us  [call(): pl.pallas_call(kernel, out_shape=out_shape, in_specs=[pl.BlockSpec(memory...]
    ppermute x2, starting transfers between devices: 2.66 us -> 3.46 us  [the longest x1 2.67 us: per_device(): across = lax.ppermute(to_across, 'gx', across_x)]
    ppermute x2, waiting for transfers between devices: 0.63 us -> 0.01 us  [the longest x1 0.01 us: per_device(): across = lax.ppermute(to_across, 'gx', across_x)]
  transfers between devices with their start and end apart: 4 -> 4, of which waited for: 1 -> 0; matrix products, arithmetic and copies ran while one was open for 0% -> 0% of each run, Pallas kernels for 13% -> 21%
where the time goes in v2:
time: 33.5 us; the launch traced here: 33.3 us
  blocking collectives  14.4 us (43%)
  Pallas kernels  11.1 us (33%)
  starting transfers between devices  6.89 us (21%)
  local copies, waits for them, and re-layouts  0.85 us (3%)
    all_to_all x1, blocking collectives, per_device(): lax.all_to_all(outgoing, ('gx', 'gy'), split_axis=0, concat_axis=0, tiled...  14.4 us
    pallas_call x5, Pallas kernels, call(): pl.pallas_call(kernel, out_shape=out_shape, in_specs=[pl.BlockSpec(memory...  11.1 us
    ppermute x1, starting transfers between devices, per_device(): across = lax.ppermute(to_across, 'gx', across_x)  2.67 us
    ppermute x1, starting transfers between devices, per_device(): from_north = lax.ppermute(before, 'gy', down_y)  2.09 us
    ppermute x1, starting transfers between devices, per_device(): from_south = lax.ppermute(after, 'gy', up_y)  1.35 us
    reshape x1, local copies, waits for them, and re-layouts, per_device(): return arrived.reshape(devices * cap, pay)  0.84 us
    ppermute x1, starting transfers between devices, per_device(): beside = lax.ppermute(to_beside, 'gx', beside_x)  0.79 us
  transfers between devices with their start and end apart: 4, of which 0 were waited for; matrix products, arithmetic and copies ran while one was open for 0% of the time, Pallas kernels for 21%

profile of v2, /device:TPU:1, one launch (start us, length us, event | category | flops | bytes accessed | tf_op | source)
XLA Modules:
  0.0 33.3 jit_solution(17233810182722252710)
XLA Ops:
  0.0 0.0 copy-start
  0.0 2.9 %shard_map.37 = (f32[2,448,128]{2,1,0:T(8,128)S(1)}, f32[2,128,128]{2,1,0:T(8,128)S(1)}, f32[8,576]{1,0:T(8,128)S(1)}, f32[8,576]{1,0:T(8,128)S(1)}, f32[3,16,80,128]{3,2,1,0:T(8,128)S(1)}) custom-call(f32[16,80,1280]{2,1,0:T(8,128)} %bitcast.3), custom_call_target="tpu_custom_call" | custom-call | tf_op jit(solution)/shard_map/pallas_call | solution.py:259
  2.9 2.7 %collective-permute-start = (f32[8,576]{1,0:T(8,128)S(1)}, f32[8,576]{1,0:T(8,128)S(1)}, u32[]{:S(2)}, u32[]{:S(2)}) collective-permute-start(f32[8,576]{1,0:T(8,128)S(1)} %get-tuple-element.20), channel_id=1, source_target_pairs={{0,28},{4,8},{8,4},{12,16},{16,12},{20,24},{24,20},{28,0},{1,29},{... | collective-permute-start | bytes 55304 | tf_op jit(solution)/shard_map/ppermute | solution.py:301
  5.5 0.8 %collective-permute-start.1 = (f32[8,576]{1,0:T(8,128)S(1)}, f32[8,576]{1,0:T(8,128)S(1)}, u32[]{:S(2)}, u32[]{:S(2)}) collective-permute-start(f32[8,576]{1,0:T(8,128)S(1)} %get-tuple-element.21), channel_id=1, source_target_pairs={{0,4},{4,0},{8,12},{12,8},{16,20},{20,16},{24,28},{28,24},{1,5},{5... | collective-permute-start | bytes 55304 | tf_op jit(solution)/shard_map/ppermute | solution.py:302
  6.3 0.0 copy-done
  6.3 2.7 %shard_map.38 = (f32[3,448,128]{2,1,0:T(8,128)S(1)}, f32[128,128]{1,0:T(8,128)S(1)}, f32[5,16,80,128]{3,2,1,0:T(8,128)S(1)}) custom-call(f32[16,80,1280]{2,1,0:T(8,128)} %bitcast.4, f32[2,128,128]{2,1,0:T(8,128)S(1)} %get-tuple-element.16.outer_edge, f32[3,16,80,128]{3,2,1,0:T(8,128)S(1)} %get-tuple-element.17.ready, f32[1280,128]{1,0:T(8,128)S(1)} %copy-done), custom_call_target="tpu_custom_call" | custom-call | tf_op jit(solution)/shard_map/pallas_call | solution.py:259
  9.1 0.0 copy-start.1
  9.1 0.0 collective-permute-done.across
  9.1 0.0 collective-permute-done.1.beside
  9.1 0.3 shard_map.40
  9.5 1.3 %collective-permute-start.2 = (f32[64,128]{1,0:T(8,128)S(1)}, f32[64,128]{1,0:T(8,128)S(1)}, u32[]{:S(2)}, u32[]{:S(2)}) collective-permute-start(f32[64,128]{1,0:T(8,128)S(1)} %get-tuple-element.23), channel_id=1, source_target_pairs={{0,1},{1,2},{2,3},{3,0},{4,5},{5,6},{6,7},{7,4},{8,9},{9,10},{10,1... | collective-permute-start | bytes 98312 | tf_op jit(solution)/shard_map/ppermute | solution.py:314
  10.8 2.1 %collective-permute-start.3 = (f32[64,128]{1,0:T(8,128)S(1)}, f32[64,128]{1,0:T(8,128)S(1)}, u32[]{:S(2)}, u32[]{:S(2)}) collective-permute-start(f32[64,128]{1,0:T(8,128)S(1)} %get-tuple-element.24), channel_id=1, source_target_pairs={{1,0},{2,1},{3,2},{0,3},{5,4},{6,5},{7,6},{4,7},{9,8},{10,9},{11,1... | collective-permute-start | bytes 98312 | tf_op jit(solution)/shard_map/ppermute | solution.py:315
  12.9 4.2 %shard_map.39.coarse = f32[448,128]{1,0:T(8,128)S(1)} custom-call(f32[2,448,128]{2,1,0:T(8,128)S(1)} %get-tuple-element.15.outer_inner, f32[3,448,128]{2,1,0:T(8,128)S(1)} %get-tuple-element.18.ready_inner, f32[5,16,80,128]{3,2,1,0:T(8,128)S(1)} %get-tuple-element.19.later, f32[1280,128]{1,0:T(8,128)S(1)} %copy-done, ...), custom_call_target="tpu_custom_call" | custom-call | tf_op jit(solution)/shard_map/pallas_call | solution.py:259
  17.1 0.0 collective-permute-done.2.south
  17.1 0.0 collective-permute-done.3.north
  17.1 0.0 copy-done.1
  17.2 0.9 %shard_map.41 = f32[32,4,640]{2,1,0:T(4,128)S(1)} custom-call(f32[448,128]{1,0:T(8,128)S(1)} %shard_map.39.coarse, f32[64,128]{1,0:T(8,128)S(1)} %collective-permute-done.2.south, f32[64,128]{1,0:T(8,128)S(1)} %collective-permute-done.3.north, s32[1,64]{1,0:T(1,128)S(1)} %bitcast.2), custom_call_target="tpu_custom_call" | custom-call | tf_op jit(solution)/shard_map/pallas_call | solution.py:259
  18.1 14.4 %all_to_all.5 = f32[32,4,640]{2,1,0:T(4,128)S(1)} all-to-all(f32[32,4,640]{2,1,0:T(4,128)S(1)} %shard_map.41), channel_id=1, replica_groups=mesh['gx'=8,'gy'=4] {'gx','gy'}, dimensions={0} | all-to-all | bytes 655360 | tf_op jit(solution)/shard_map/all_to_all | solution.py:340
  32.5 0.8 %reshape.11 = f32[128,640]{1,0:T(8,128)} reshape(f32[32,4,640]{2,1,0:T(4,128)S(1)} %all_to_all.5) | data formatting | bytes 655360 | tf_op jit(solution)/shard_map/reshape | solution.py:341
Async XLA Ops:
  0.0 6.3 %copy-start = (f32[1280,128]{1,0:T(8,128)S(1)}, f32[1280,128]{1,0:T(8,128)}, u32[]{:S(2)}) copy-start(f32[1280,128]{1,0:T(8,128)} %constant.2.clone.weights) | copy-start | bytes 1966084
  2.9 6.2 %collective-permute-start = (f32[8,576]{1,0:T(8,128)S(1)}, f32[8,576]{1,0:T(8,128)S(1)}, u32[]{:S(2)}, u32[]{:S(2)}) collective-permute-start(f32[8,576]{1,0:T(8,128)S(1)} %get-tuple-element.20), channel_id=1, source_target_pairs={{0,28},{4,8},{8,4},{12,16},{16,12},{20,24},{24,20},{28,0},{1,29},{... | collective-permute-start | bytes 55304 | tf_op jit(solution)/shard_map/ppermute | solution.py:301
  5.5 3.6 %collective-permute-start.1 = (f32[8,576]{1,0:T(8,128)S(1)}, f32[8,576]{1,0:T(8,128)S(1)}, u32[]{:S(2)}, u32[]{:S(2)}) collective-permute-start(f32[8,576]{1,0:T(8,128)S(1)} %get-tuple-element.21), channel_id=1, source_target_pairs={{0,4},{4,0},{8,12},{12,8},{16,20},{20,16},{24,28},{28,24},{1,5},{5... | collective-permute-start | bytes 55304 | tf_op jit(solution)/shard_map/ppermute | solution.py:302
  9.1 8.1 %copy-start.1 = (s32[64,1]{0,1:T(1,128)S(1)}, s32[64,1]{0,1:T(1,128)}, u32[]{:S(2)}) copy-start(s32[64,1]{0,1:T(1,128)} %param.4) | copy-start | bytes 772
  9.5 7.7 %collective-permute-start.2 = (f32[64,128]{1,0:T(8,128)S(1)}, f32[64,128]{1,0:T(8,128)S(1)}, u32[]{:S(2)}, u32[]{:S(2)}) collective-permute-start(f32[64,128]{1,0:T(8,128)S(1)} %get-tuple-element.23), channel_id=1, source_target_pairs={{0,1},{1,2},{2,3},{3,0},{4,5},{5,6},{6,7},{7,4},{8,9},{9,10},{10,1... | collective-permute-start | bytes 98312 | tf_op jit(solution)/shard_map/ppermute | solution.py:314
  10.8 6.3 %collective-permute-start.3 = (f32[64,128]{1,0:T(8,128)S(1)}, f32[64,128]{1,0:T(8,128)S(1)}, u32[]{:S(2)}, u32[]{:S(2)}) collective-permute-start(f32[64,128]{1,0:T(8,128)S(1)} %get-tuple-element.24), channel_id=1, source_target_pairs={{1,0},{2,1},{3,2},{0,3},{5,4},{6,5},{7,6},{4,7},{9,8},{10,9},{11,1... | collective-permute-start | bytes 98312 | tf_op jit(solution)/shard_map/ppermute | solution.py:315

commit v3 on v2

--- a/solution.py
+++ b/solution.py
@@ -2,6 +2,7 @@
 
 import jax
 import jax.numpy as jnp
+import ml_dtypes
 import numpy as np
 from jax import lax
 from jax.experimental import pallas as pl
@@ -43,12 +44,28 @@
     return np.where(inside, TAPS[np.clip(tap, 0, 20)], np.float32(0))
 
 
-def beyond_weights(side):
-    row = lax.broadcasted_iota(jnp.int32, (8, LANES), 0)
-    lane = lax.broadcasted_iota(jnp.int32, (8, LANES), 1)
-    weights = jnp.zeros((8, LANES), jnp.float32)
-    for at, tap in enumerate(G[15:21]) if side == 0 else enumerate(G[0:5], LANES - 5):
-        weights = jnp.where((row == 0) & (lane == at), tap, weights)
+def split(values):
+    parts = []
+    for _ in range(3):
+        part = values.astype(ml_dtypes.bfloat16)
+        parts.append(part)
+        values = values - part.astype(np.float32)
+    return parts
+
+
+def split_weights(columns, order):
+    tiles = east_weights(columns).reshape(-1, LANES, columns // RATIO)
+    first, second, third = split(tiles[list(order)].reshape(columns, -1))
+    return np.concatenate([first, second], axis=1), third
+
+
+def beyond_weights():
+    row = lax.broadcasted_iota(jnp.int32, (16, LANES), 0)
+    lane = lax.broadcasted_iota(jnp.int32, (16, LANES), 1)
+    weights = jnp.zeros((16, LANES), jnp.float32)
+    for side, taps in ((0, enumerate(G[15:21])), (8, enumerate(G[0:5], LANES - 5))):
+        for at, tap in taps:
+            weights = jnp.where((row == side) & (lane == at), tap, weights)
     return weights
 
 
@@ -85,7 +102,7 @@
 
 
 def strided(tile, level, p):
-    return [tile[c * LEVELS + level, pl.ds(p, ROWS, stride=RATIO), :] for c in range(COMPONENTS)]
+    return [tile[c, level, pl.ds(p, ROWS, stride=RATIO), :] for c in range(COMPONENTS)]
 
 
 def sublane_sums(values):
@@ -110,25 +127,24 @@
 
 
 def end_sums(tile, edge):
-    last = tile.shape[1] - ROWS
+    last = tile.shape[2] - ROWS
     for side, start in enumerate((0, last)):
         taps = end_taps(side)
         for level in range(LEVELS):
-            values = [tile[c * LEVELS + level, pl.ds(start, ROWS), :] for c in range(COMPONENTS)]
+            values = [tile[c, level, pl.ds(start, ROWS), :] for c in range(COMPONENTS)]
             terms = weighed(values, taps, None)
             place = side * EDGE + level * PADDED
             edge[pl.ds(place, ROWS), :] = sublane_sums(terms[:ROWS])
             edge[pl.ds(place + ROWS, ROWS), :] = sublane_sums(terms[ROWS:] + terms[: 2 * ROWS - TERMS])
 
 
-def filter_tile(tile, inner, edge=None):
-    for level in range(LEVELS):
-        inside, below, above = north_sums(functools.partial(strided, tile, level))
-        for q in range(TERMS):
-            inner[pl.ds((q * LEVELS + level) * ROWS, ROWS), :] = inside[q]
-            if edge is not None:
-                edge[pl.ds(level * PADDED + q, 1), :] = below[q][0:1]
-                edge[pl.ds(EDGE + level * PADDED + q, 1), :] = above[q][ROWS - 1 : ROWS]
+def filter_level(tile, level, inner, edge=None):
+    inside, below, above = north_sums(functools.partial(strided, tile, level))
+    for q in range(TERMS):
+        inner[pl.ds((q * LEVELS + level) * ROWS, ROWS), :] = inside[q]
+        if edge is not None:
+            edge[pl.ds(level * PADDED + q, 1), :] = below[q][0:1]
+            edge[pl.ds(EDGE + level * PADDED + q, 1), :] = above[q][ROWS - 1 : ROWS]
 
 
 def clear_padding(edge):
@@ -138,57 +154,89 @@
 
 def tile_copies(fields, places, sems):
     return [
-        pltpu.make_async_copy(fields.at[:, :, pl.ds(t * LANES, LANES)], place, sems.at[i])
+        pltpu.make_async_copy(fields.at[:, :, :, pl.ds(t * LANES, LANES)], place, sems.at[i])
         for i, (t, place) in enumerate(places)
     ]
 
 
-def outer_kernel(order, fields, inner, edge, across, beside, ready, tile, sems):
-    places = [(t, tile.at[i] if i < OUTER else ready.at[i - OUTER]) for i, t in enumerate(order[: OUTER + READY])]
-    copies = tile_copies(fields, places, sems)
-    for copy in copies:
+def outer_kernel(order, fields, inner, edge, across, beside, ready, tile, level_sems, sems):
+    arriving = [
+        [
+            pltpu.make_async_copy(
+                fields.at[:, level, :, pl.ds(order[i] * LANES, LANES)], tile.at[i, :, level], level_sems.at[i, level]
+            )
+            for level in range(LEVELS)
+        ]
+        for i in range(OUTER)
+    ]
+    copies = tile_copies(fields, [(t, ready.at[i]) for i, t in enumerate(order[OUTER : OUTER + READY])], sems)
+    for copy in arriving[0] + arriving[1] + copies:
         copy.start()
-    messages = []
     for i in range(OUTER):
         clear_padding(edge.at[i])
-        copies[i].wait()
-        filter_tile(tile.at[i], inner.at[i], edge.at[i])
-        sums = jnp.concatenate([inner[i], edge[i]], axis=0)
-        messages.append(
-            lax.dot_general(
-                beyond_weights(i), sums, (((1,), (1,)), ((), ())), precision=HIGHEST, preferred_element_type=jnp.float32
-            )
-        )
+        for level in range(LEVELS):
+            arriving[i][level].wait()
+            filter_level(tile.at[i], level, inner.at[i], edge.at[i])
+    lane = lax.broadcasted_iota(jnp.int32, (1, LANES), 1)
+    first, last = (jnp.concatenate([inner[i], edge[i]], axis=0) for i in range(OUTER))
+    beyond = jnp.concatenate(split_here(beyond_weights()), axis=0)
+    total = None
+    for part in split_here(jnp.where(lane < LANES // 2, first, last)):
+        sums = lax.dot_general(beyond, part, (((1,), (1,)), ((), ())), preferred_element_type=jnp.float32)
+        total = sums if total is None else total + sums
+    messages = total[:16] + (total[16:32] + total[32:])
     odd = lax.axis_index("gx") % 2 == 1
-    across[...] = jnp.where(odd, messages[1], messages[0])
-    beside[...] = jnp.where(odd, messages[0], messages[1])
-    for copy in copies[OUTER:]:
+    across[...] = jnp.where(odd, messages[8:], messages[:8])
+    beside[...] = jnp.where(odd, messages[:8], messages[8:])
+    for copy in copies:
         copy.wait()
 
 
-def middle_kernel(order, fields, outer_edge, ready, weights, inner, partial, later, edge, sems):
+def split_here(values):
+    first = values.astype(jnp.bfloat16)
+    left = values - first.astype(jnp.float32)
+    second = left.astype(jnp.bfloat16)
+    return first, second, (left - second.astype(jnp.float32)).astype(jnp.bfloat16)
+
+
+def dot(a, b):
+    return jnp.dot(a, b, preferred_element_type=jnp.float32)
+
+
+def east_sums(values, pair, weights, third):
+    rows = pl.ds(pair * 2 * LANES, 2 * LANES)
+    a, b, c = split_here(values)
+    both = dot(a, weights[rows, :]) + dot(b, weights[rows, :])
+    small = dot(a, third[rows, :]) + dot(c, weights[rows, :LANES])
+    return both[:, :LANES] + (both[:, LANES:] + small)
+
+
+def middle_kernel(order, fields, outer_edge, ready, weights, third, inner, partial, later, edge, sems):
     count = len(order) - OUTER - READY
     copies = tile_copies(fields, [(t, later.at[i]) for i, t in enumerate(order[OUTER + READY :])], sems)
     for copy in copies:
         copy.start()
-    for i in range(READY):
+    tiles = [outer_edge.at[i] for i in range(OUTER)] + [edge.at[i] for i in range(READY + count)]
+
+    def add(pair):
+        both = jnp.concatenate([tiles[2 * pair][...], tiles[2 * pair + 1][...]], axis=1)
+        part = east_sums(both, pair, weights, third)
+        partial[...] = part if pair == 0 else partial[...] + part
+
+    done = 0
+    for i in range(READY + count):
         clear_padding(edge.at[i])
-        filter_tile(ready.at[i], inner.at[i], edge.at[i])
-    for i in range(count):
-        copies[i].wait()
-        end_sums(later.at[i], edge.at[READY + i])
-    tiles = [outer_edge[i] for i in range(OUTER)] + [edge[i] for i in range(READY + count)]
-    partial[...] = east_sums(order, tiles, weights)
-
-
-def east_sums(order, tiles, weights):
-    total = None
-    for i in range(0, len(order), 2):
-        pair = jnp.concatenate(tiles[i : i + 2], axis=1)
-        rows = jnp.concatenate([weights[t * LANES : (t + 1) * LANES, :] for t in order[i : i + 2]], axis=0)
-        part = jnp.dot(pair, rows, precision=HIGHEST, preferred_element_type=jnp.float32)
-        total = part if total is None else total + part
-    return total
+        if i < READY:
+            for level in range(LEVELS):
+                filter_level(ready.at[i], level, inner.at[i], edge.at[i])
+        else:
+            copies[i - READY].wait()
+            end_sums(later.at[i - READY], edge.at[i])
+        if 2 * done + 2 <= OUTER + i:
+            add(done)
+            done += 1
+    for pair in range(done, len(order) // 2):
+        add(pair)
 
 
 def from_sides(across, beside):
@@ -205,14 +253,26 @@
     after[...] = total[EDGE:]
 
 
-def coarse_kernel(order, outer_inner, ready_inner, later, weights, across, beside, coarse, inner):
+def coarse_kernel(outer_inner, ready_inner, later, weights, third, across, beside, coarse, inner):
     count = later.shape[0]
+    tiles = [outer_inner.at[i] for i in range(OUTER)] + [ready_inner.at[i] for i in range(READY)]
+    tiles += [inner.at[i] for i in range(count)]
+    stop = TERMS * LEVELS * ROWS
+    coarse[...] = from_sides(across[:, :stop], beside[:, :stop])
+
+    def add(pair):
+        both = jnp.concatenate([tiles[2 * pair][...], tiles[2 * pair + 1][...]], axis=1)
+        coarse[...] += east_sums(both, pair, weights, third)
+
+    done = 0
     for i in range(count):
-        filter_tile(later.at[i], inner.at[i])
-    tiles = [outer_inner[i] for i in range(OUTER)] + [ready_inner[i] for i in range(READY)]
-    tiles += [inner[i] for i in range(count)]
-    stop = TERMS * LEVELS * ROWS
-    coarse[...] = east_sums(order, tiles, weights) + from_sides(across[:, :stop], beside[:, :stop])
+        if 2 * done + 2 <= OUTER + READY + i:
+            add(done)
+            done += 1
+        for level in range(LEVELS):
+            filter_level(later.at[i], level, inner.at[i])
+    for pair in range(done, len(tiles) // 2):
+        add(pair)
 
 
 def send_kernel(cap, coarse, south, north, owner, outgoing, filtered, spread):
@@ -237,18 +297,19 @@
     named = jnp.broadcast_to(column, (blocks, LANES))
     slot_row = lax.broadcasted_iota(jnp.int32, (slots, LANES), 0)
     stresses = spread[...].reshape(len(PRODUCT_PAIRS) * LEVELS, blocks // across, BLK * BLK, LANES)
-    total = None
+    picks, payloads = [], []
     for by in range(blocks // across):
         block = by * across + lax.broadcasted_iota(jnp.int32, (blocks, LANES), 1) // BLK
         mine = jnp.sum(jnp.where(index == block, named, 0), axis=0, keepdims=True)
         earlier = jnp.where((index < block) & (named == mine), 1, 0)
         slot = mine * cap + jnp.sum(earlier, axis=0, keepdims=True)
-        chosen = jnp.where(slot_row == slot, 1.0, 0.0)
-        payload = stresses[:, by].reshape(-1, LANES)
-        part = lax.dot_general(
-            chosen, payload, (((1,), (1,)), ((), ())), precision=HIGHEST, preferred_element_type=jnp.float32
-        )
-        total = part if total is None else total + part
+        picks.append(jnp.where(slot_row == slot, 1.0, 0.0).astype(jnp.bfloat16))
+        payloads.append(stresses[:, by].reshape(-1, LANES))
+    chosen = jnp.concatenate(picks, axis=1)
+    total = None
+    for part in split_here(jnp.concatenate(payloads, axis=1)):
+        sums = lax.dot_general(chosen, part, (((1,), (1,)), ((), ())), preferred_element_type=jnp.float32)
+        total = sums if total is None else total + sums
     for d in range(outgoing.shape[0]):
         outgoing[d] = total[d * cap : (d + 1) * cap]
 
@@ -274,10 +335,9 @@
     _, _, height, width = fields.shape
     tiles = width // LANES
     rows = TERMS * LEVELS * ROWS
-    fine = COMPONENTS * LEVELS
-    flat = fields.reshape(fine, height, width)
-    weights = jnp.asarray(east_weights(width))
+    lane_tile = (COMPONENTS, LEVELS, height, LANES)
     order = (0, tiles - 1) + tuple(range(1, tiles - 1))
+    weights, third = [jnp.asarray(w) for w in split_weights(width, order)]
     rest = tiles - OUTER - READY
     message = f32(8, rows + 2 * EDGE)
     outer_inner, outer_edge, to_across, to_beside, ready = call(
@@ -287,10 +347,14 @@
             f32(OUTER, 2 * EDGE, LANES),
             message,
             message,
-            f32(READY, fine, height, LANES),
+            f32(READY, *lane_tile),
         ),
-        flat,
-        scratch=[pltpu.VMEM((OUTER, fine, height, LANES), jnp.float32), pltpu.SemaphoreType.DMA((OUTER + READY,))],
+        fields,
+        scratch=[
+            pltpu.VMEM((OUTER, *lane_tile), jnp.float32),
+            pltpu.SemaphoreType.DMA((OUTER, LEVELS)),
+            pltpu.SemaphoreType.DMA((READY,)),
+        ],
         hbm=1,
     )
     nx, ny = lax.axis_size("gx"), lax.axis_size("gy")
@@ -302,11 +366,12 @@
     beside = lax.ppermute(to_beside, "gx", beside_x)
     ready_inner, partial, later = call(
         functools.partial(middle_kernel, order),
-        (f32(READY, rows, LANES), f32(2 * EDGE, LANES), f32(rest, fine, height, LANES)),
-        flat,
+        (f32(READY, rows, LANES), f32(2 * EDGE, LANES), f32(rest, *lane_tile)),
+        fields,
         outer_edge,
         ready,
         weights,
+        third,
         scratch=[pltpu.VMEM((READY + rest, 2 * EDGE, LANES), jnp.float32), pltpu.SemaphoreType.DMA((rest,))],
         hbm=1,
     )
@@ -314,12 +379,13 @@
     from_south = lax.ppermute(after, "gy", up_y)
     from_north = lax.ppermute(before, "gy", down_y)
     coarse = call(
-        functools.partial(coarse_kernel, order),
+        coarse_kernel,
         f32(rows, LANES),
         outer_inner,
         ready_inner,
         later,
         weights,
+        third,
         across,
         beside,
         scratch=[pltpu.VMEM((rest, rows, LANES), jnp.float32)],

time: 33.5 us -> 32.1 us (0.958)
  Pallas kernels: 11.1 us -> 9.21 us
  blocking collectives: 14.4 us -> 14.9 us
    pallas_call x5, Pallas kernels: 11.1 us -> 9.21 us  [call(): pl.pallas_call(kernel, out_shape=out_shape, in_specs=[pl.BlockSpec(memory...]
    all_to_all x1, blocking collectives: 14.4 us -> 14.9 us  [per_device(): lax.all_to_all(outgoing, ('gx', 'gy'), split_axis=0, concat_axis=0, tiled...]
  transfers between devices with their start and end apart: 4 -> 4, of which waited for: 0 -> 0; matrix products, arithmetic and copies ran while one was open for 0% -> 0% of each run, Pallas kernels for 21% -> 19%
where the time goes in v3:
time: 32.1 us; the launch traced here: 32 us
  blocking collectives  14.9 us (46%)
  Pallas kernels  9.21 us (29%)
  starting transfers between devices  6.9 us (21%)
  local copies, waits for them, and re-layouts  0.85 us (3%)
    all_to_all x1, blocking collectives, per_device(): lax.all_to_all(outgoing, ('gx', 'gy'), split_axis=0, concat_axis=0, tiled...  14.9 us
    pallas_call x5, Pallas kernels, call(): pl.pallas_call(kernel, out_shape=out_shape, in_specs=[pl.BlockSpec(memory...  9.21 us
    ppermute x1, starting transfers between devices, per_device(): across = lax.ppermute(to_across, 'gx', across_x)  2.67 us
    ppermute x1, starting transfers between devices, per_device(): from_north = lax.ppermute(before, 'gy', down_y)  2.09 us
    ppermute x1, starting transfers between devices, per_device(): from_south = lax.ppermute(after, 'gy', up_y)  1.35 us
    reshape x1, local copies, waits for them, and re-layouts, per_device(): return arrived.reshape(devices * cap, pay)  0.84 us
    ppermute x1, starting transfers between devices, per_device(): beside = lax.ppermute(to_beside, 'gx', beside_x)  0.79 us
  transfers between devices with their start and end apart: 4, of which 0 were waited for; matrix products, arithmetic and copies ran while one was open for 0% of the time, Pallas kernels for 19%

profile of v3, /device:TPU:1, one launch (start us, length us, event | category | flops | bytes accessed | tf_op | source)
XLA Modules:
  0.0 32.0 jit_solution(6412361586208322518)
XLA Ops:
  0.0 0.0 copy-start
  0.0 0.0 copy-start.1
  0.0 2.3 %shard_map.46 = (f32[2,448,128]{2,1,0:T(8,128)S(1)}, f32[2,128,128]{2,1,0:T(8,128)S(1)}, f32[8,576]{1,0:T(8,128)S(1)}, f32[8,576]{1,0:T(8,128)S(1)}, f32[3,4,4,80,128]{4,3,2,1,0:T(8,128)S(1)}) custom-call(f32[4,4,80,1280]{3,2,1,0:T(8,128)} %fields.3), custom_call_target="tpu_custom_call" | custom-call | tf_op jit(solution)/shard_map/pallas_call | solution.py:320
  2.3 2.7 %collective-permute-start = (f32[8,576]{1,0:T(8,128)S(1)}, f32[8,576]{1,0:T(8,128)S(1)}, u32[]{:S(2)}, u32[]{:S(2)}) collective-permute-start(f32[8,576]{1,0:T(8,128)S(1)} %get-tuple-element.20), channel_id=1, source_target_pairs={{0,28},{4,8},{8,4},{12,16},{16,12},{20,24},{24,20},{28,0},{1,29},{... | collective-permute-start | bytes 55304 | tf_op jit(solution)/shard_map/ppermute | solution.py:365
  4.9 0.8 %collective-permute-start.1 = (f32[8,576]{1,0:T(8,128)S(1)}, f32[8,576]{1,0:T(8,128)S(1)}, u32[]{:S(2)}, u32[]{:S(2)}) collective-permute-start(f32[8,576]{1,0:T(8,128)S(1)} %get-tuple-element.21), channel_id=1, source_target_pairs={{0,4},{4,0},{8,12},{12,8},{16,20},{20,16},{24,28},{28,24},{1,5},{5... | collective-permute-start | bytes 55304 | tf_op jit(solution)/shard_map/ppermute | solution.py:366
  5.7 0.0 copy-done
  5.7 0.0 copy-done.1
  5.7 2.4 %shard_map.47 = (f32[3,448,128]{2,1,0:T(8,128)S(1)}, f32[128,128]{1,0:T(8,128)S(1)}, f32[5,4,4,80,128]{4,3,2,1,0:T(8,128)S(1)}) custom-call(f32[4,4,80,1280]{3,2,1,0:T(8,128)} %fields.3, f32[2,128,128]{2,1,0:T(8,128)S(1)} %get-tuple-element.16.outer_edge, f32[3,4,4,80,128]{4,3,2,1,0:T(8,128)S(1)} %get-tuple-element.17.ready, bf16[1280,256]{1,0:T(8,128)(2,1)S(1)} %copy-done, ...), custom_call_target="tpu_custom_call" | custom-call | tf_op jit(solution)/shard_map/pallas_call | solution.py:320
  8.2 0.0 copy-start.2
  8.2 0.0 collective-permute-done.across
  8.2 0.0 collective-permute-done.1.beside
  8.2 0.3 %shard_map.49 = (f32[64,128]{1,0:T(8,128)S(1)}, f32[64,128]{1,0:T(8,128)S(1)}) custom-call(f32[128,128]{1,0:T(8,128)S(1)} %get-tuple-element.22.partial, f32[8,576]{1,0:T(8,128)S(1)} %collective-permute-done.across, f32[8,576]{1,0:T(8,128)S(1)} %collective-permute-done.1.beside), custom_call_target="tpu_custom_call" | custom-call | tf_op jit(solution)/shard_map/pallas_call | solution.py:320
  8.5 1.4 %collective-permute-start.2 = (f32[64,128]{1,0:T(8,128)S(1)}, f32[64,128]{1,0:T(8,128)S(1)}, u32[]{:S(2)}, u32[]{:S(2)}) collective-permute-start(f32[64,128]{1,0:T(8,128)S(1)} %get-tuple-element.23), channel_id=1, source_target_pairs={{0,1},{1,2},{2,3},{3,0},{4,5},{5,6},{6,7},{7,4},{8,9},{9,10},{10,1... | collective-permute-start | bytes 98312 | tf_op jit(solution)/shard_map/ppermute | solution.py:379
  9.9 2.1 %collective-permute-start.3 = (f32[64,128]{1,0:T(8,128)S(1)}, f32[64,128]{1,0:T(8,128)S(1)}, u32[]{:S(2)}, u32[]{:S(2)}) collective-permute-start(f32[64,128]{1,0:T(8,128)S(1)} %get-tuple-element.24), channel_id=1, source_target_pairs={{1,0},{2,1},{3,2},{0,3},{5,4},{6,5},{7,6},{4,7},{9,8},{10,9},{11,1... | collective-permute-start | bytes 98312 | tf_op jit(solution)/shard_map/ppermute | solution.py:380
  12.0 3.6 %shard_map.48.coarse = f32[448,128]{1,0:T(8,128)S(1)} custom-call(f32[2,448,128]{2,1,0:T(8,128)S(1)} %get-tuple-element.15.outer_inner, f32[3,448,128]{2,1,0:T(8,128)S(1)} %get-tuple-element.18.ready_inner, f32[5,4,4,80,128]{4,3,2,1,0:T(8,128)S(1)} %get-tuple-element.19.later, bf16[1280,256]{1,0:T(8,128)(2,1)S(1)} %copy-done, ...), custom_call_target="tpu_custom_call" | custom-call | tf_op jit(solution)/shard_map/pallas_call | solution.py:320
  15.6 0.0 collective-permute-done.2.south
  15.6 0.0 collective-permute-done.3.north
  15.6 0.0 copy-done.2
  15.6 0.6 %shard_map.50 = f32[32,4,640]{2,1,0:T(4,128)S(1)} custom-call(f32[448,128]{1,0:T(8,128)S(1)} %shard_map.48.coarse, f32[64,128]{1,0:T(8,128)S(1)} %collective-permute-done.2.south, f32[64,128]{1,0:T(8,128)S(1)} %collective-permute-done.3.north, s32[1,64]{1,0:T(1,128)S(1)} %bitcast.1), custom_call_target="tpu_custom_call" | custom-call | tf_op jit(solution)/shard_map/pallas_call | solution.py:320
  16.2 14.9 %all_to_all.5 = f32[32,4,640]{2,1,0:T(4,128)S(1)} all-to-all(f32[32,4,640]{2,1,0:T(4,128)S(1)} %shard_map.50), channel_id=1, replica_groups=mesh['gx'=8,'gy'=4] {'gx','gy'}, dimensions={0} | all-to-all | bytes 655360 | tf_op jit(solution)/shard_map/all_to_all | solution.py:406
  31.1 0.8 %reshape.7 = f32[128,640]{1,0:T(8,128)} reshape(f32[32,4,640]{2,1,0:T(4,128)S(1)} %all_to_all.5) | data formatting | bytes 655360 | tf_op jit(solution)/shard_map/reshape | solution.py:407
Async XLA Ops:
  0.0 5.7 %copy-start = (bf16[1280,256]{1,0:T(8,128)(2,1)S(1)}, bf16[1280,256]{1,0:T(8,128)(2,1)}, u32[]{:S(2)}) copy-start(bf16[1280,256]{1,0:T(8,128)(2,1)} %constant.4.clone.weights) | copy-start | bytes 1966084
  0.0 5.7 %copy-start.1 = (bf16[1280,128]{1,0:T(8,128)(2,1)S(1)}, bf16[1280,128]{1,0:T(8,128)(2,1)}, u32[]{:S(2)}) copy-start(bf16[1280,128]{1,0:T(8,128)(2,1)} %constant.5.clone.third) | copy-start | bytes 983044
  2.3 5.9 %collective-permute-start = (f32[8,576]{1,0:T(8,128)S(1)}, f32[8,576]{1,0:T(8,128)S(1)}, u32[]{:S(2)}, u32[]{:S(2)}) collective-permute-start(f32[8,576]{1,0:T(8,128)S(1)} %get-tuple-element.20), channel_id=1, source_target_pairs={{0,28},{4,8},{8,4},{12,16},{16,12},{20,24},{24,20},{28,0},{1,29},{... | collective-permute-start | bytes 55304 | tf_op jit(solution)/shard_map/ppermute | solution.py:365
  4.9 3.3 %collective-permute-start.1 = (f32[8,576]{1,0:T(8,128)S(1)}, f32[8,576]{1,0:T(8,128)S(1)}, u32[]{:S(2)}, u32[]{:S(2)}) collective-permute-start(f32[8,576]{1,0:T(8,128)S(1)} %get-tuple-element.21), channel_id=1, source_target_pairs={{0,4},{4,0},{8,12},{12,8},{16,20},{20,16},{24,28},{28,24},{1,5},{5... | collective-permute-start | bytes 55304 | tf_op jit(solution)/shard_map/ppermute | solution.py:366
  8.2 7.4 %copy-start.2 = (s32[64,1]{0,1:T(1,128)S(1)}, s32[64,1]{0,1:T(1,128)}, u32[]{:S(2)}) copy-start(s32[64,1]{0,1:T(1,128)} %param.5) | copy-start | bytes 772
  8.5 7.0 %collective-permute-start.2 = (f32[64,128]{1,0:T(8,128)S(1)}, f32[64,128]{1,0:T(8,128)S(1)}, u32[]{:S(2)}, u32[]{:S(2)}) collective-permute-start(f32[64,128]{1,0:T(8,128)S(1)} %get-tuple-element.23), channel_id=1, source_target_pairs={{0,1},{1,2},{2,3},{3,0},{4,5},{5,6},{6,7},{7,4},{8,9},{9,10},{10,1... | collective-permute-start | bytes 98312 | tf_op jit(solution)/shard_map/ppermute | solution.py:379
  9.9 5.7 %collective-permute-start.3 = (f32[64,128]{1,0:T(8,128)S(1)}, f32[64,128]{1,0:T(8,128)S(1)}, u32[]{:S(2)}, u32[]{:S(2)}) collective-permute-start(f32[64,128]{1,0:T(8,128)S(1)} %get-tuple-element.24), channel_id=1, source_target_pairs={{1,0},{2,1},{3,2},{0,3},{5,4},{6,5},{7,6},{4,7},{9,8},{10,9},{11,1... | collective-permute-start | bytes 98312 | tf_op jit(solution)/shard_map/ppermute | solution.py:380

commit v4 on v3

v4 whole, which is shorter than its diff:
```python
import functools

import jax
import jax.numpy as jnp
import ml_dtypes
import numpy as np
from jax import lax
from jax.experimental import pallas as pl
from jax.experimental.pallas import tpu as pltpu
from jax.sharding import PartitionSpec as P

BLK = 4
RATIO = 10
LANES = 128
HIGHEST = lax.Precision.HIGHEST
SIGMA_CELLS = 2.8867513
PRODUCT_PAIRS = ((0, 0), (0, 1), (0, 2), (0, 3), (1, 1), (1, 2), (1, 3), (2, 2), (2, 3), (3, 3))
COMPONENTS = 4
TERMS = COMPONENTS + len(PRODUCT_PAIRS)
LEVELS = 4
ROWS = 8
OUTER = 2
BROUGHT = 4
FULL = 5
EDGE = TERMS * LEVELS
VMEM_BYTES = 16 * 1024 * 1024


def gauss_taps():
    spread = np.arange(21, dtype=np.float64) - 10.0
    values = np.exp(-spread * spread / (2.0 * SIGMA_CELLS * SIGMA_CELLS))
    return (values / values.sum()).astype(np.float32)


TAPS = gauss_taps()
G = [float(v) for v in TAPS]


def east_weights(columns):
    fine = np.arange(columns)[:, None]
    coarse = np.arange(columns // RATIO)[None, :]
    tap = fine - RATIO * coarse + 5
    inside = (tap >= 0) & (tap <= 20)
    return np.where(inside, TAPS[np.clip(tap, 0, 20)], np.float32(0))


def split(values):
    parts = []
    for _ in range(3):
        part = values.astype(ml_dtypes.bfloat16)
        parts.append(part)
        values = values - part.astype(np.float32)
    return parts


def split_weights(columns, order):
    tiles = east_weights(columns).reshape(-1, LANES, columns // RATIO)
    first, second, third = split(tiles[list(order)].reshape(columns, -1))
    return np.concatenate([first, second], axis=1), third


def beyond_weights():
    row = lax.broadcasted_iota(jnp.int32, (16, LANES), 0)
    lane = lax.broadcasted_iota(jnp.int32, (16, LANES), 1)
    weights = jnp.zeros((16, LANES), jnp.float32)
    for side, taps in ((0, enumerate(G[15:21])), (8, enumerate(G[0:5], LANES - 5))):
        for at, tap in taps:
            weights = jnp.where((row == side) & (lane == at), tap, weights)
    return weights


def edge_places():
    odd = lax.axis_index("gx") % 2
    row = lax.broadcasted_iota(jnp.int32, (ROWS, LANES), 0)
    lane = lax.broadcasted_iota(jnp.int32, (ROWS, LANES), 1)
    across = odd * (LANES - 1)
    return jnp.where((row == 0) & (lane == across) | (row == 1) & (lane == LANES - 1 - across), 1.0, 0.0)


def weighed(values, weight):
    scaled = [v * weight for v in values]
    return scaled + [scaled[a] * values[b] for a, b in PRODUCT_PAIRS]


def added(sums, terms):
    return [s + t for s, t in zip(sums, terms)]


def strided(tile, level, p):
    start = level * (tile.shape[1] // LEVELS) + p
    return [tile[c, pl.ds(start, ROWS, stride=RATIO), :] for c in range(COMPONENTS)]


def end_sums(tile, edge):
    height = tile.shape[1] // LEVELS
    row = lax.broadcasted_iota(jnp.int32, (ROWS, LANES), 0)
    total = None
    for p in range(6):
        ends = (pl.ds(p, LEVELS, stride=height), pl.ds(height - 6 + p, LEVELS, stride=height))
        values = [jnp.concatenate([tile[c, end, :] for end in ends], axis=0) for c in range(COMPONENTS)]
        terms = weighed(values, jnp.where(row < LEVELS, G[p + 15], G[p - 1] if p else 0.0))
        total = terms if total is None else added(total, terms)
    for q, value in enumerate(total):
        edge[pl.ds(q * ROWS, ROWS), :] = value


GROUPS = ((0, 1, 2, 3, 4, 5, 6, 7), (8, 9, 10, 11, 12, 13))


def filter_level(load, level, inner, edge=None):
    for group in GROUPS:

        def terms_of(p, weight):
            values = load(level, p)
            scaled = [v * weight for v in values]
            pairs = [PRODUCT_PAIRS[q - COMPONENTS] if q >= COMPONENTS else (q, None) for q in group]
            return [scaled[a] if b is None else scaled[a] * values[b] for a, b in pairs]

        own = below = terms_of(0, G[5])
        for p in range(1, 5):
            own = added(own, terms_of(p, G[p + 5]))
            below = added(below, terms_of(p, G[p + 15]))
        own = added(own, terms_of(5, G[10]))
        above = terms_of(5, G[0])
        below = added(below, above)
        if edge is not None:
            for q, value in zip(group, below):
                edge[pl.ds(q * ROWS + level, 1), :] = value[0:1]
        own = [o + pltpu.roll(v, ROWS - 1, 0) for o, v in zip(own, below)]
        for p in range(6, RATIO):
            own = added(own, terms_of(p, G[p + 5]))
            above = added(above, terms_of(p, G[p - 5]))
        for q, o, value in zip(group, own, above):
            inner[pl.ds((q * LEVELS + level) * ROWS, ROWS), :] = o + pltpu.roll(value, 1, 0)
            if edge is not None:
                edge[pl.ds(q * ROWS + LEVELS + level, 1), :] = value[ROWS - 1 : ROWS]


def tile_copies(fields, places, sems):
    return [
        pltpu.make_async_copy(fields.at[:, :, pl.ds(t * LANES, LANES)], place, sems.at[i])
        for i, (t, place) in enumerate(places)
    ]


def outer_kernel(order, fields, across, beside, ready, inner, edge, level_sems, sems):
    height = fields.shape[1] // LEVELS
    arriving = []
    for level in range(LEVELS):
        rows = pl.ds(level * height, height)
        arriving.append(
            [
                pltpu.make_async_copy(
                    fields.at[:, rows, pl.ds(order[i] * LANES, LANES)], ready.at[i, :, rows], level_sems.at[i, level]
                )
                for i in range(OUTER)
            ]
        )
    copies = tile_copies(fields, [(order[i], ready.at[i]) for i in range(OUTER, BROUGHT)], sems)
    for copy in sum(arriving, []) + copies:
        copy.start()
    lane = lax.broadcasted_iota(jnp.int32, (ROWS, LANES), 1)

    def merged(level, p):
        first, last = (strided(ready.at[i], level, p) for i in range(OUTER))
        return [jnp.where(lane < LANES // 2, f, s) for f, s in zip(first, last)]

    for level in range(LEVELS):
        for copy in arriving[level]:
            copy.wait()
        filter_level(merged, level, inner, edge)
    beyond = jnp.concatenate(split_here(beyond_weights()), axis=0)
    total = None
    for part in split_here(jnp.concatenate([inner[...], edge[...]], axis=0)):
        sums = lax.dot_general(beyond, part, (((1,), (1,)), ((), ())), preferred_element_type=jnp.float32)
        total = sums if total is None else total + sums
    messages = total[:16] + (total[16:32] + total[32:])
    odd = lax.axis_index("gx") % 2 == 1
    across[...] = jnp.where(odd, messages[8:9], messages[:1])
    beside[...] = jnp.where(odd, messages[:1], messages[8:9])
    for copy in copies:
        copy.wait()


def split_here(values):
    first = values.astype(jnp.bfloat16)
    left = values - first.astype(jnp.float32)
    second = left.astype(jnp.bfloat16)
    return first, second, (left - second.astype(jnp.float32)).astype(jnp.bfloat16)


def dot(a, b):
    return jnp.dot(a, b, preferred_element_type=jnp.float32)


def east_sums(values, pair, weights, third):
    rows = pl.ds(pair * 2 * LANES, 2 * LANES)
    a, b, c = split_here(values)
    both = dot(a, weights[rows, :]) + dot(b, weights[rows, :])
    small = dot(a, third[rows, :]) + dot(c, weights[rows, :LANES])
    return both[:, :LANES] + (both[:, LANES:] + small)


def middle_kernel(order, fields, ready, weights, third, inner, partial, later, tile, edge, sems):
    places = [tile.at[i] for i in range(FULL - BROUGHT)] + [later.at[i] for i in range(len(order) - FULL)]
    copies = tile_copies(fields, list(zip(order[BROUGHT:], places)), sems)
    for copy in copies:
        copy.start()
    tiles = [ready.at[i] for i in range(BROUGHT)] + places

    def add(pair):
        both = jnp.concatenate([edge[2 * pair], edge[2 * pair + 1]], axis=1)
        part = east_sums(both, pair, weights, third)
        partial[...] = part if pair == 0 else partial[...] + part

    for i in range(len(order)):
        if i >= BROUGHT:
            copies[i - BROUGHT].wait()
        if i < FULL:
            for level in range(LEVELS):
                filter_level(functools.partial(strided, tiles[i]), level, inner.at[i], edge.at[i])
        else:
            end_sums(tiles[i], edge.at[i])
    for pair in range(len(order) // 2):
        add(pair)


def from_sides(across, beside):
    none = jnp.zeros((ROWS - 2, across.shape[1]), jnp.float32)
    both = jnp.concatenate([across, beside, none], axis=0)
    return lax.dot_general(
        both, edge_places(), (((0,), (0,)), ((), ())), precision=HIGHEST, preferred_element_type=jnp.float32
    )


def corner_kernel(partial, across, beside, before, after):
    start = TERMS * LEVELS * ROWS
    total = partial[...] + from_sides(across[:, start:], beside[:, start:])
    for q in range(TERMS):
        rows = pl.ds(q * LEVELS, LEVELS)
        before[rows, :] = total[q * ROWS : q * ROWS + LEVELS]
        after[rows, :] = total[q * ROWS + LEVELS : (q + 1) * ROWS]


def coarse_kernel(full_inner, later, weights, third, across, beside, coarse, inner):
    count = later.shape[0]
    tiles = [full_inner.at[i] for i in range(FULL)] + [inner.at[i] for i in range(count)]
    stop = TERMS * LEVELS * ROWS
    coarse[...] = from_sides(across[:, :stop], beside[:, :stop])

    def add(pair):
        both = jnp.concatenate([tiles[2 * pair][...], tiles[2 * pair + 1][...]], axis=1)
        coarse[...] += east_sums(both, pair, weights, third)

    done = 0
    for i in range(count):
        if 2 * done + 2 <= FULL + i:
            add(done)
            done += 1
        for level in range(LEVELS):
            filter_level(functools.partial(strided, later.at[i]), level, inner.at[i])
    for pair in range(done, len(tiles) // 2):
        add(pair)


def send_kernel(cap, coarse, south, north, before, after, owner, outgoing, filtered, spread):
    filtered[...] = coarse[...]
    slab = LEVELS * ROWS
    filtered[pl.ds(0, EDGE, stride=ROWS), :] += south[...] - after[...]
    filtered[pl.ds(ROWS - 1, EDGE, stride=ROWS), :] += north[...] - before[...]
    means = [filtered[c * slab : (c + 1) * slab, :] for c in range(COMPONENTS)]
    lane = lax.broadcasted_iota(jnp.int32, (slab, LANES), 1) % BLK
    for k, (a, b) in enumerate(PRODUCT_PAIRS):
        q = COMPONENTS + k
        stress = filtered[q * slab : (q + 1) * slab, :] - means[a] * means[b]
        for c in range(BLK):
            spread[pl.ds(k * slab * BLK + c, slab, stride=BLK), :] = jnp.where(lane == c, stress, 0.0)
    slots = outgoing.shape[0] * outgoing.shape[1]
    blocks = owner.shape[1]
    across = LANES // BLK
    own = lax.broadcasted_iota(jnp.int32, (blocks, blocks), 0) == lax.broadcasted_iota(jnp.int32, (blocks, blocks), 1)
    column = jnp.sum(jnp.where(own, jnp.broadcast_to(owner[...], (blocks, blocks)), 0), axis=1, keepdims=True)
    index = lax.broadcasted_iota(jnp.int32, (blocks, LANES), 0)
    named = jnp.broadcast_to(column, (blocks, LANES))
    slot_row = lax.broadcasted_iota(jnp.int32, (slots, LANES), 0)
    stresses = spread[...].reshape(len(PRODUCT_PAIRS) * LEVELS, blocks // across, BLK * BLK, LANES)
    picks, payloads = [], []
    for by in range(blocks // across):
        block = by * across + lax.broadcasted_iota(jnp.int32, (blocks, LANES), 1) // BLK
        mine = jnp.sum(jnp.where(index == block, named, 0), axis=0, keepdims=True)
        earlier = jnp.where((index < block) & (named == mine), 1, 0)
        slot = mine * cap + jnp.sum(earlier, axis=0, keepdims=True)
        picks.append(jnp.where(slot_row == slot, 1.0, 0.0).astype(jnp.bfloat16))
        payloads.append(stresses[:, by].reshape(-1, LANES))
    chosen = jnp.concatenate(picks, axis=1)
    total = None
    for part in split_here(jnp.concatenate(payloads, axis=1)):
        sums = lax.dot_general(chosen, part, (((1,), (1,)), ((), ())), preferred_element_type=jnp.float32)
        total = sums if total is None else total + sums
    for d in range(outgoing.shape[0]):
        outgoing[d] = total[d * cap : (d + 1) * cap]


def call(kernel, out_shape, *args, scratch=(), hbm=0):
    whole = pl.BlockSpec(memory_space=pltpu.VMEM)
    held = [pltpu.with_memory_space_constraint(a, pltpu.VMEM if i >= hbm else pltpu.HBM) for i, a in enumerate(args)]
    return pl.pallas_call(
        kernel,
        out_shape=out_shape,
        in_specs=[pl.BlockSpec(memory_space=pltpu.HBM)] * hbm + [whole] * (len(args) - hbm),
        out_specs=jax.tree.map(lambda _: whole, out_shape),
        scratch_shapes=list(scratch),
        compiler_params=pltpu.CompilerParams(vmem_limit_bytes=VMEM_BYTES),
    )(*held)


def f32(*shape):
    return jax.ShapeDtypeStruct(shape, jnp.float32)


def per_device(fields, owner):
    _, _, height, width = fields.shape
    tiles = width // LANES
    rows = TERMS * LEVELS * ROWS
    flat = fields.reshape(COMPONENTS, LEVELS * height, width)
    lane_tile = (COMPONENTS, LEVELS * height, LANES)
    order = (0, tiles - 1) + tuple(range(1, tiles - 1))
    weights, third = [jnp.asarray(w) for w in split_weights(width, order)]
    rest = tiles - FULL
    message = f32(1, rows + 2 * EDGE)
    to_across, to_beside, ready = call(
        functools.partial(outer_kernel, order),
        (message, message, f32(BROUGHT, *lane_tile)),
        flat,
        scratch=[
            pltpu.VMEM((rows, LANES), jnp.float32),
            pltpu.VMEM((2 * EDGE, LANES), jnp.float32),
            pltpu.SemaphoreType.DMA((OUTER, LEVELS)),
            pltpu.SemaphoreType.DMA((BROUGHT - OUTER,)),
        ],
        hbm=1,
    )
    nx, ny = lax.axis_size("gx"), lax.axis_size("gy")
    beside_x = [(i, i ^ 1) for i in range(nx)]
    across_x = [(i, (i + 1) % nx if i % 2 else (i - 1) % nx) for i in range(nx)]
    up_y = [(i, (i + 1) % ny) for i in range(ny)]
    down_y = [(j, i) for i, j in up_y]
    across = lax.ppermute(to_across, "gx", across_x)
    beside = lax.ppermute(to_beside, "gx", beside_x)
    full_inner, partial, later = call(
        functools.partial(middle_kernel, order),
        (f32(FULL, rows, LANES), f32(2 * EDGE, LANES), f32(rest, *lane_tile)),
        flat,
        ready,
        weights,
        third,
        scratch=[
            pltpu.VMEM((FULL - BROUGHT, *lane_tile), jnp.float32),
            pltpu.VMEM((tiles, 2 * EDGE, LANES), jnp.float32),
            pltpu.SemaphoreType.DMA((tiles - BROUGHT,)),
        ],
        hbm=1,
    )
    before, after = call(corner_kernel, (f32(EDGE, LANES), f32(EDGE, LANES)), partial, across, beside)
    from_south = lax.ppermute(after, "gy", up_y)
    from_north = lax.ppermute(before, "gy", down_y)
    coarse = call(
        coarse_kernel,
        f32(rows, LANES),
        full_inner,
        later,
        weights,
        third,
        across,
        beside,
        scratch=[pltpu.VMEM((rest, rows, LANES), jnp.float32)],
    )
    devices = nx * ny
    blocks = owner.shape[0]
    cap = max(2, 2 * blocks // devices)
    pay = len(PRODUCT_PAIRS) * LEVELS * BLK * BLK
    outgoing = call(
        functools.partial(send_kernel, cap),
        f32(devices, cap, pay),
        coarse,
        from_south,
        from_north,
        before,
        after,
        owner.reshape(1, blocks),
        scratch=[pltpu.VMEM((rows, LANES), jnp.float32), pltpu.VMEM((pay * blocks * BLK // LANES, LANES), jnp.float32)],
    )
    arrived = lax.all_to_all(outgoing, ("gx", "gy"), split_axis=0, concat_axis=0, tiled=True)
    return arrived.reshape(devices * cap, pay)


def solution(mesh):
    placed = (P(None, None, "gy", "gx"), P(("gx", "gy"), None))
    return jax.shard_map(
        per_device, mesh=mesh, in_specs=placed, out_specs=P(("gx", "gy"), None), check_vma=False
    )
```

time: 32.1 us -> 31.8 us (level)
  no operation moved by 1% of the time
where the time goes in v4:
time: 31.8 us; the launch traced here: 31.7 us
  blocking collectives  14.8 us (47%)
  Pallas kernels  8.99 us (28%)
  starting transfers between devices  6.89 us (22%)
  local copies, waits for them, and re-layouts  0.85 us (3%)
    all_to_all x1, blocking collectives, per_device(): lax.all_to_all(outgoing, ('gx', 'gy'), split_axis=0, concat_axis=0, tiled...  14.8 us
    pallas_call x5, Pallas kernels, call(): pl.pallas_call(kernel, out_shape=out_shape, in_specs=[pl.BlockSpec(memory...  8.99 us
    ppermute x1, starting transfers between devices, per_device(): across = lax.ppermute(to_across, 'gx', across_x)  2.67 us
    ppermute x1, starting transfers between devices, per_device(): from_north = lax.ppermute(before, 'gy', down_y)  2.09 us
    ppermute x1, starting transfers between devices, per_device(): from_south = lax.ppermute(after, 'gy', up_y)  1.35 us
    reshape x1, local copies, waits for them, and re-layouts, per_device(): return arrived.reshape(devices * cap, pay)  0.84 us
    ppermute x1, starting transfers between devices, per_device(): beside = lax.ppermute(to_beside, 'gx', beside_x)  0.79 us
  transfers between devices with their start and end apart: 4, of which 0 were waited for; matrix products, arithmetic and copies ran while one was open for 0% of the time, Pallas kernels for 19%

profile of v4, /device:TPU:1, one launch (start us, length us, event | category | flops | bytes accessed | tf_op | source)
XLA Modules:
  0.0 31.7 jit_solution(9663941583575706940)
XLA Ops:
  0.0 0.0 copy-start
  0.0 0.0 copy-start.1
  0.0 2.0 %shard_map.46 = (f32[1,560]{1,0:T(1,128)S(1)}, f32[1,560]{1,0:T(1,128)S(1)}, f32[4,4,320,128]{3,2,1,0:T(8,128)S(1)}) custom-call(f32[4,320,1280]{2,1,0:T(8,128)} %bitcast.3), custom_call_target="tpu_custom_call" | custom-call | tf_op jit(solution)/shard_map/pallas_call | solution.py:307
  2.0 2.7 %collective-permute-start = (f32[1,560]{1,0:T(1,128)S(1)}, f32[1,560]{1,0:T(1,128)S(1)}, u32[]{:S(2)}, u32[]{:S(2)}) collective-permute-start(f32[1,560]{1,0:T(1,128)S(1)} %get-tuple-element.16), channel_id=1, source_target_pairs={{0,28},{4,8},{8,4},{12,16},{16,12},{20,24},{24,20},{28,0},{1,29},{... | collective-permute-start | bytes 6728 | tf_op jit(solution)/shard_map/ppermute | solution.py:348
  4.7 0.8 %collective-permute-start.1 = (f32[1,560]{1,0:T(1,128)S(1)}, f32[1,560]{1,0:T(1,128)S(1)}, u32[]{:S(2)}, u32[]{:S(2)}) collective-permute-start(f32[1,560]{1,0:T(1,128)S(1)} %get-tuple-element.17), channel_id=1, source_target_pairs={{0,4},{4,0},{8,12},{12,8},{16,20},{20,16},{24,28},{28,24},{1,5},{5... | collective-permute-start | bytes 6728 | tf_op jit(solution)/shard_map/ppermute | solution.py:349
  5.5 0.0 copy-done
  5.5 0.0 copy-done.1
  5.5 2.7 %shard_map.47 = (f32[5,448,128]{2,1,0:T(8,128)S(1)}, f32[112,128]{1,0:T(8,128)S(1)}, f32[5,4,320,128]{3,2,1,0:T(8,128)S(1)}) custom-call(f32[4,320,1280]{2,1,0:T(8,128)} %bitcast.4, f32[4,4,320,128]{3,2,1,0:T(8,128)S(1)} %get-tuple-element.13.ready, bf16[1280,256]{1,0:T(8,128)(2,1)S(1)} %copy-done, bf16[1280,128]{1,0:T(8,128)(2,1)S(1)} %copy-done.1), custom_call_target="tpu_custom_call" | custom-call | tf_op jit(solution)/shard_map/pallas_call | solution.py:307
  8.2 0.0 copy-start.2
  8.2 0.0 collective-permute-done.across
  8.2 0.0 collective-permute-done.1.beside
  8.2 0.3 %shard_map.49 = (f32[56,128]{1,0:T(8,128)S(1)}, f32[56,128]{1,0:T(8,128)S(1)}) custom-call(f32[112,128]{1,0:T(8,128)S(1)} %get-tuple-element.18.partial, f32[1,560]{1,0:T(1,128)S(1)} %collective-permute-done.across, f32[1,560]{1,0:T(1,128)S(1)} %collective-permute-done.1.beside), custom_call_target="tpu_custom_call" | custom-call | tf_op jit(solution)/shard_map/pallas_call | solution.py:307
  8.5 1.4 %collective-permute-start.2 = (f32[56,128]{1,0:T(8,128)S(1)}, f32[56,128]{1,0:T(8,128)S(1)}, u32[]{:S(2)}, u32[]{:S(2)}) collective-permute-start(f32[56,128]{1,0:T(8,128)S(1)} %get-tuple-element.19.after), channel_id=1, source_target_pairs={{0,1},{1,2},{2,3},{3,0},{4,5},{5,6},{6,7},{7,4},{8,9},{9,10},{10,1... | collective-permute-start | bytes 86024 | tf_op jit(solution)/shard_map/ppermute | solution.py:365
  9.9 2.1 %collective-permute-start.3 = (f32[56,128]{1,0:T(8,128)S(1)}, f32[56,128]{1,0:T(8,128)S(1)}, u32[]{:S(2)}, u32[]{:S(2)}) collective-permute-start(f32[56,128]{1,0:T(8,128)S(1)} %get-tuple-element.20.before), channel_id=1, source_target_pairs={{1,0},{2,1},{3,2},{0,3},{5,4},{6,5},{7,6},{4,7},{9,8},{10,9},{11,1... | collective-permute-start | bytes 86024 | tf_op jit(solution)/shard_map/ppermute | solution.py:366
  12.0 3.4 %shard_map.48.coarse = f32[448,128]{1,0:T(8,128)S(1)} custom-call(f32[5,448,128]{2,1,0:T(8,128)S(1)} %get-tuple-element.14.full_inner, f32[5,4,320,128]{3,2,1,0:T(8,128)S(1)} %get-tuple-element.15.later, bf16[1280,256]{1,0:T(8,128)(2,1)S(1)} %copy-done, bf16[1280,128]{1,0:T(8,128)(2,1)S(1)} %copy-done.1, f32[1,560]{1,0:T(1,128)S(1)} %collective-permute-done.across, ...), custom_call_target="tpu_custom_call" | custom-call | tf_op jit(solution)/shard_map/pallas_call | solution.py:307
  15.4 0.0 collective-permute-done.2.south
  15.4 0.0 collective-permute-done.3.north
  15.4 0.0 copy-done.2
  15.4 0.6 %shard_map.50 = f32[32,4,640]{2,1,0:T(4,128)S(1)} custom-call(f32[448,128]{1,0:T(8,128)S(1)} %shard_map.48.coarse, f32[56,128]{1,0:T(8,128)S(1)} %collective-permute-done.2.south, f32[56,128]{1,0:T(8,128)S(1)} %collective-permute-done.3.north, f32[56,128]{1,0:T(8,128)S(1)} %get-tuple-element.20.before, f32[56,128]{1,0:T(8,128)S(1)} %get-tuple-element.19.after, ...), custom_call_target="tpu_custom_call" | custom-call | tf_op jit(solution)/shard_map/pallas_call | solution.py:307
  16.0 14.8 %all_to_all.5 = f32[32,4,640]{2,1,0:T(4,128)S(1)} all-to-all(f32[32,4,640]{2,1,0:T(4,128)S(1)} %shard_map.50), channel_id=1, replica_groups=mesh['gx'=8,'gy'=4] {'gx','gy'}, dimensions={0} | all-to-all | bytes 655360 | tf_op jit(solution)/shard_map/all_to_all | solution.py:393
  30.8 0.8 %reshape.11 = f32[128,640]{1,0:T(8,128)} reshape(f32[32,4,640]{2,1,0:T(4,128)S(1)} %all_to_all.5) | data formatting | bytes 655360 | tf_op jit(solution)/shard_map/reshape | solution.py:394
Async XLA Ops:
  0.0 5.5 %copy-start = (bf16[1280,256]{1,0:T(8,128)(2,1)S(1)}, bf16[1280,256]{1,0:T(8,128)(2,1)}, u32[]{:S(2)}) copy-start(bf16[1280,256]{1,0:T(8,128)(2,1)} %constant.4.clone.weights) | copy-start | bytes 1966084
  0.0 5.5 %copy-start.1 = (bf16[1280,128]{1,0:T(8,128)(2,1)S(1)}, bf16[1280,128]{1,0:T(8,128)(2,1)}, u32[]{:S(2)}) copy-start(bf16[1280,128]{1,0:T(8,128)(2,1)} %constant.5.clone.third) | copy-start | bytes 983044
  2.0 6.2 %collective-permute-start = (f32[1,560]{1,0:T(1,128)S(1)}, f32[1,560]{1,0:T(1,128)S(1)}, u32[]{:S(2)}, u32[]{:S(2)}) collective-permute-start(f32[1,560]{1,0:T(1,128)S(1)} %get-tuple-element.16), channel_id=1, source_target_pairs={{0,28},{4,8},{8,4},{12,16},{16,12},{20,24},{24,20},{28,0},{1,29},{... | collective-permute-start | bytes 6728 | tf_op jit(solution)/shard_map/ppermute | solution.py:348
  4.7 3.5 %collective-permute-start.1 = (f32[1,560]{1,0:T(1,128)S(1)}, f32[1,560]{1,0:T(1,128)S(1)}, u32[]{:S(2)}, u32[]{:S(2)}) collective-permute-start(f32[1,560]{1,0:T(1,128)S(1)} %get-tuple-element.17), channel_id=1, source_target_pairs={{0,4},{4,0},{8,12},{12,8},{16,20},{20,16},{24,28},{28,24},{1,5},{5... | collective-permute-start | bytes 6728 | tf_op jit(solution)/shard_map/ppermute | solution.py:349
  8.2 7.2 %copy-start.2 = (s32[64,1]{0,1:T(1,128)S(1)}, s32[64,1]{0,1:T(1,128)}, u32[]{:S(2)}) copy-start(s32[64,1]{0,1:T(1,128)} %param.5) | copy-start | bytes 772
  8.5 6.8 %collective-permute-start.2 = (f32[56,128]{1,0:T(8,128)S(1)}, f32[56,128]{1,0:T(8,128)S(1)}, u32[]{:S(2)}, u32[]{:S(2)}) collective-permute-start(f32[56,128]{1,0:T(8,128)S(1)} %get-tuple-element.19.after), channel_id=1, source_target_pairs={{0,1},{1,2},{2,3},{3,0},{4,5},{5,6},{6,7},{7,4},{8,9},{9,10},{10,1... | collective-permute-start | bytes 86024 | tf_op jit(solution)/shard_map/ppermute | solution.py:365
  9.9 5.5 %collective-permute-start.3 = (f32[56,128]{1,0:T(8,128)S(1)}, f32[56,128]{1,0:T(8,128)S(1)}, u32[]{:S(2)}, u32[]{:S(2)}) collective-permute-start(f32[56,128]{1,0:T(8,128)S(1)} %get-tuple-element.20.before), channel_id=1, source_target_pairs={{1,0},{2,1},{3,2},{0,3},{5,4},{6,5},{7,6},{4,7},{9,8},{10,9},{11,1... | collective-permute-start | bytes 86024 | tf_op jit(solution)/shard_map/ppermute | solution.py:366

commit v5 on v4

--- a/solution.py
+++ b/solution.py
@@ -301,14 +301,32 @@
         outgoing[d] = total[d * cap : (d + 1) * cap]
 
 
-def call(kernel, out_shape, *args, scratch=(), hbm=0):
+def place_kernel(arrived, received, rows, sems):
+    parts = rows.shape[0]
+    sources, cap, _ = arrived.shape
+    count = sources // parts
+    copies = []
+    for part in range(parts):
+        for d in range(count):
+            rows[part, pl.ds(d * cap, cap), :] = arrived[part * count + d]
+        copies.append(
+            pltpu.make_async_copy(
+                rows.at[part], received.at[pl.ds(part * count * cap, count * cap), :], sems.at[part]
+            )
+        )
+        copies[-1].start()
+    for copy in copies:
+        copy.wait()
+
+
+def call(kernel, out_shape, *args, scratch=(), hbm=0, out=pltpu.VMEM):
     whole = pl.BlockSpec(memory_space=pltpu.VMEM)
     held = [pltpu.with_memory_space_constraint(a, pltpu.VMEM if i >= hbm else pltpu.HBM) for i, a in enumerate(args)]
     return pl.pallas_call(
         kernel,
         out_shape=out_shape,
         in_specs=[pl.BlockSpec(memory_space=pltpu.HBM)] * hbm + [whole] * (len(args) - hbm),
-        out_specs=jax.tree.map(lambda _: whole, out_shape),
+        out_specs=jax.tree.map(lambda _: pl.BlockSpec(memory_space=out), out_shape),
         scratch_shapes=list(scratch),
         compiler_params=pltpu.CompilerParams(vmem_limit_bytes=VMEM_BYTES),
     )(*held)
@@ -391,7 +409,14 @@
         scratch=[pltpu.VMEM((rows, LANES), jnp.float32), pltpu.VMEM((pay * blocks * BLK // LANES, LANES), jnp.float32)],
     )
     arrived = lax.all_to_all(outgoing, ("gx", "gy"), split_axis=0, concat_axis=0, tiled=True)
-    return arrived.reshape(devices * cap, pay)
+    parts = 4
+    return call(
+        place_kernel,
+        f32(devices * cap, pay),
+        arrived,
+        scratch=[pltpu.VMEM((parts, devices * cap // parts, pay), jnp.float32), pltpu.SemaphoreType.DMA((parts,))],
+        out=pltpu.HBM,
+    )
 
 
 def solution(mesh):

time: 31.8 us -> 31.7 us (level)
  local copies, waits for them, and re-layouts: 0.85 us -> 0.01 us
  Pallas kernels: 8.99 us -> 9.75 us
    reshape x1 -> x0, local copies, waits for them, and re-layouts: 0.84 us -> none  [per_device(): return arrived.reshape(devices * cap, pay)]
    pallas_call x5 -> x6, Pallas kernels: 8.99 us -> 9.75 us  [call(): pl.pallas_call(kernel, out_shape=out_shape, in_specs=[pl.BlockSpec(memory...]
where the time goes in v5:
time: 31.7 us; the launch traced here: 31.6 us
  blocking collectives  14.8 us (47%)
  Pallas kernels  9.75 us (31%)
  starting transfers between devices  6.89 us (22%)
    all_to_all x1, blocking collectives, per_device(): lax.all_to_all(outgoing, ('gx', 'gy'), split_axis=0, concat_axis=0, tiled...  14.8 us
    pallas_call x6, Pallas kernels, call(): pl.pallas_call(kernel, out_shape=out_shape, in_specs=[pl.BlockSpec(memory...  9.75 us
    ppermute x1, starting transfers between devices, per_device(): across = lax.ppermute(to_across, 'gx', across_x)  2.67 us
    ppermute x1, starting transfers between devices, per_device(): from_north = lax.ppermute(before, 'gy', down_y)  2.09 us
    ppermute x1, starting transfers between devices, per_device(): from_south = lax.ppermute(after, 'gy', up_y)  1.35 us
    ppermute x1, starting transfers between devices, per_device(): beside = lax.ppermute(to_beside, 'gx', beside_x)  0.79 us
  transfers between devices with their start and end apart: 4, of which 0 were waited for; matrix products, arithmetic and copies ran while one was open for 0% of the time, Pallas kernels for 19%

profile of v5, /device:TPU:1, one launch (start us, length us, event | category | flops | bytes accessed | tf_op | source)
XLA Modules:
  0.0 31.6 jit_solution(4851605557330615530)
XLA Ops:
  0.0 0.0 copy-start
  0.0 0.0 copy-start.1
  0.0 2.0 %shard_map.46 = (f32[1,560]{1,0:T(1,128)S(1)}, f32[1,560]{1,0:T(1,128)S(1)}, f32[4,4,320,128]{3,2,1,0:T(8,128)S(1)}) custom-call(f32[4,320,1280]{2,1,0:T(8,128)} %bitcast.3), custom_call_target="tpu_custom_call" | custom-call | tf_op jit(solution)/shard_map/pallas_call | solution.py:325
  2.0 2.7 %collective-permute-start = (f32[1,560]{1,0:T(1,128)S(1)}, f32[1,560]{1,0:T(1,128)S(1)}, u32[]{:S(2)}, u32[]{:S(2)}) collective-permute-start(f32[1,560]{1,0:T(1,128)S(1)} %get-tuple-element.16), channel_id=1, source_target_pairs={{0,28},{4,8},{8,4},{12,16},{16,12},{20,24},{24,20},{28,0},{1,29},{... | collective-permute-start | bytes 6728 | tf_op jit(solution)/shard_map/ppermute | solution.py:366
  4.7 0.8 %collective-permute-start.1 = (f32[1,560]{1,0:T(1,128)S(1)}, f32[1,560]{1,0:T(1,128)S(1)}, u32[]{:S(2)}, u32[]{:S(2)}) collective-permute-start(f32[1,560]{1,0:T(1,128)S(1)} %get-tuple-element.17), channel_id=1, source_target_pairs={{0,4},{4,0},{8,12},{12,8},{16,20},{20,16},{24,28},{28,24},{1,5},{5... | collective-permute-start | bytes 6728 | tf_op jit(solution)/shard_map/ppermute | solution.py:367
  5.5 0.0 copy-done
  5.5 0.0 copy-done.1
  5.5 2.7 %shard_map.47 = (f32[5,448,128]{2,1,0:T(8,128)S(1)}, f32[112,128]{1,0:T(8,128)S(1)}, f32[5,4,320,128]{3,2,1,0:T(8,128)S(1)}) custom-call(f32[4,320,1280]{2,1,0:T(8,128)} %bitcast.4, f32[4,4,320,128]{3,2,1,0:T(8,128)S(1)} %get-tuple-element.13.ready, bf16[1280,256]{1,0:T(8,128)(2,1)S(1)} %copy-done, bf16[1280,128]{1,0:T(8,128)(2,1)S(1)} %copy-done.1), custom_call_target="tpu_custom_call" | custom-call | tf_op jit(solution)/shard_map/pallas_call | solution.py:325
  8.2 0.0 copy-start.2
  8.2 0.0 collective-permute-done.across
  8.2 0.0 collective-permute-done.1.beside
  8.2 0.3 %shard_map.49 = (f32[56,128]{1,0:T(8,128)S(1)}, f32[56,128]{1,0:T(8,128)S(1)}) custom-call(f32[112,128]{1,0:T(8,128)S(1)} %get-tuple-element.18.partial, f32[1,560]{1,0:T(1,128)S(1)} %collective-permute-done.across, f32[1,560]{1,0:T(1,128)S(1)} %collective-permute-done.1.beside), custom_call_target="tpu_custom_call" | custom-call | tf_op jit(solution)/shard_map/pallas_call | solution.py:325
  8.5 1.4 %collective-permute-start.2 = (f32[56,128]{1,0:T(8,128)S(1)}, f32[56,128]{1,0:T(8,128)S(1)}, u32[]{:S(2)}, u32[]{:S(2)}) collective-permute-start(f32[56,128]{1,0:T(8,128)S(1)} %get-tuple-element.19.after), channel_id=1, source_target_pairs={{0,1},{1,2},{2,3},{3,0},{4,5},{5,6},{6,7},{7,4},{8,9},{9,10},{10,1... | collective-permute-start | bytes 86024 | tf_op jit(solution)/shard_map/ppermute | solution.py:383
  9.9 2.1 %collective-permute-start.3 = (f32[56,128]{1,0:T(8,128)S(1)}, f32[56,128]{1,0:T(8,128)S(1)}, u32[]{:S(2)}, u32[]{:S(2)}) collective-permute-start(f32[56,128]{1,0:T(8,128)S(1)} %get-tuple-element.20.before), channel_id=1, source_target_pairs={{1,0},{2,1},{3,2},{0,3},{5,4},{6,5},{7,6},{4,7},{9,8},{10,9},{11,1... | collective-permute-start | bytes 86024 | tf_op jit(solution)/shard_map/ppermute | solution.py:384
  12.0 3.4 %shard_map.48.coarse = f32[448,128]{1,0:T(8,128)S(1)} custom-call(f32[5,448,128]{2,1,0:T(8,128)S(1)} %get-tuple-element.14.full_inner, f32[5,4,320,128]{3,2,1,0:T(8,128)S(1)} %get-tuple-element.15.later, bf16[1280,256]{1,0:T(8,128)(2,1)S(1)} %copy-done, bf16[1280,128]{1,0:T(8,128)(2,1)S(1)} %copy-done.1, f32[1,560]{1,0:T(1,128)S(1)} %collective-permute-done.across, ...), custom_call_target="tpu_custom_call" | custom-call | tf_op jit(solution)/shard_map/pallas_call | solution.py:325
  15.4 0.0 collective-permute-done.2.south
  15.4 0.0 collective-permute-done.3.north
  15.4 0.0 copy-done.2
  15.4 0.6 %shard_map.50 = f32[32,4,640]{2,1,0:T(4,128)S(1)} custom-call(f32[448,128]{1,0:T(8,128)S(1)} %shard_map.48.coarse, f32[56,128]{1,0:T(8,128)S(1)} %collective-permute-done.2.south, f32[56,128]{1,0:T(8,128)S(1)} %collective-permute-done.3.north, f32[56,128]{1,0:T(8,128)S(1)} %get-tuple-element.20.before, f32[56,128]{1,0:T(8,128)S(1)} %get-tuple-element.19.after, ...), custom_call_target="tpu_custom_call" | custom-call | tf_op jit(solution)/shard_map/pallas_call | solution.py:325
  16.0 14.8 %all_to_all.5.arrived = f32[32,4,640]{2,1,0:T(4,128)S(1)} all-to-all(f32[32,4,640]{2,1,0:T(4,128)S(1)} %shard_map.50), channel_id=1, replica_groups=mesh['gx'=8,'gy'=4] {'gx','gy'}, dimensions={0} | all-to-all | bytes 655360 | tf_op jit(solution)/shard_map/all_to_all | solution.py:411
  30.8 0.8 %shard_map.51 = f32[128,640]{1,0:T(8,128)} custom-call(f32[32,4,640]{2,1,0:T(4,128)S(1)} %all_to_all.5.arrived), custom_call_target="tpu_custom_call" | custom-call | tf_op jit(solution)/shard_map/pallas_call | solution.py:325
Async XLA Ops:
  0.0 5.5 %copy-start = (bf16[1280,256]{1,0:T(8,128)(2,1)S(1)}, bf16[1280,256]{1,0:T(8,128)(2,1)}, u32[]{:S(2)}) copy-start(bf16[1280,256]{1,0:T(8,128)(2,1)} %constant.4.clone.weights) | copy-start | bytes 1966084
  0.0 5.5 %copy-start.1 = (bf16[1280,128]{1,0:T(8,128)(2,1)S(1)}, bf16[1280,128]{1,0:T(8,128)(2,1)}, u32[]{:S(2)}) copy-start(bf16[1280,128]{1,0:T(8,128)(2,1)} %constant.5.clone.third) | copy-start | bytes 983044
  2.0 6.2 %collective-permute-start = (f32[1,560]{1,0:T(1,128)S(1)}, f32[1,560]{1,0:T(1,128)S(1)}, u32[]{:S(2)}, u32[]{:S(2)}) collective-permute-start(f32[1,560]{1,0:T(1,128)S(1)} %get-tuple-element.16), channel_id=1, source_target_pairs={{0,28},{4,8},{8,4},{12,16},{16,12},{20,24},{24,20},{28,0},{1,29},{... | collective-permute-start | bytes 6728 | tf_op jit(solution)/shard_map/ppermute | solution.py:366
  4.7 3.5 %collective-permute-start.1 = (f32[1,560]{1,0:T(1,128)S(1)}, f32[1,560]{1,0:T(1,128)S(1)}, u32[]{:S(2)}, u32[]{:S(2)}) collective-permute-start(f32[1,560]{1,0:T(1,128)S(1)} %get-tuple-element.17), channel_id=1, source_target_pairs={{0,4},{4,0},{8,12},{12,8},{16,20},{20,16},{24,28},{28,24},{1,5},{5... | collective-permute-start | bytes 6728 | tf_op jit(solution)/shard_map/ppermute | solution.py:367
  8.2 7.2 %copy-start.2 = (s32[64,1]{0,1:T(1,128)S(1)}, s32[64,1]{0,1:T(1,128)}, u32[]{:S(2)}) copy-start(s32[64,1]{0,1:T(1,128)} %param.5) | copy-start | bytes 772
  8.5 6.8 %collective-permute-start.2 = (f32[56,128]{1,0:T(8,128)S(1)}, f32[56,128]{1,0:T(8,128)S(1)}, u32[]{:S(2)}, u32[]{:S(2)}) collective-permute-start(f32[56,128]{1,0:T(8,128)S(1)} %get-tuple-element.19.after), channel_id=1, source_target_pairs={{0,1},{1,2},{2,3},{3,0},{4,5},{5,6},{6,7},{7,4},{8,9},{9,10},{10,1... | collective-permute-start | bytes 86024 | tf_op jit(solution)/shard_map/ppermute | solution.py:383
  9.9 5.5 %collective-permute-start.3 = (f32[56,128]{1,0:T(8,128)S(1)}, f32[56,128]{1,0:T(8,128)S(1)}, u32[]{:S(2)}, u32[]{:S(2)}) collective-permute-start(f32[56,128]{1,0:T(8,128)S(1)} %get-tuple-element.20.before), channel_id=1, source_target_pairs={{1,0},{2,1},{3,2},{0,3},{5,4},{6,5},{7,6},{4,7},{9,8},{10,9},{11,1... | collective-permute-start | bytes 86024 | tf_op jit(solution)/shard_map/ppermute | solution.py:384

commit v6 on v5

--- a/solution.py
+++ b/solution.py
@@ -32,8 +32,25 @@
     return (values / values.sum()).astype(np.float32)
 
 
+def two_parts(value):
+    first = np.float64(ml_dtypes.bfloat16(value))
+    return first + np.float64(ml_dtypes.bfloat16(value - first))
+
+
+def rounded_taps(taps):
+    taps = taps.astype(np.float64)
+    taps, rounded = taps / taps.sum(), np.zeros(21)
+    rounded[10] = two_parts(taps[10])
+    left = taps[10] - rounded[10]
+    for t in range(9, -1, -1):
+        rounded[t] = rounded[20 - t] = two_parts(taps[t] + left / 2)
+        left += 2 * (taps[t] - rounded[t])
+    return rounded.astype(np.float32)
+
+
 TAPS = gauss_taps()
 G = [float(v) for v in TAPS]
+EAST = rounded_taps(TAPS)
 
 
 def east_weights(columns):
@@ -41,31 +58,23 @@
     coarse = np.arange(columns // RATIO)[None, :]
     tap = fine - RATIO * coarse + 5
     inside = (tap >= 0) & (tap <= 20)
-    return np.where(inside, TAPS[np.clip(tap, 0, 20)], np.float32(0))
-
-
-def split(values):
-    parts = []
-    for _ in range(3):
-        part = values.astype(ml_dtypes.bfloat16)
-        parts.append(part)
-        values = values - part.astype(np.float32)
-    return parts
+    return np.where(inside, EAST[np.clip(tap, 0, 20)], np.float32(0))
 
 
 def split_weights(columns, order):
     tiles = east_weights(columns).reshape(-1, LANES, columns // RATIO)
-    first, second, third = split(tiles[list(order)].reshape(columns, -1))
-    return np.concatenate([first, second], axis=1), third
+    weights = tiles[list(order)].reshape(columns, -1)
+    first = weights.astype(ml_dtypes.bfloat16)
+    return np.concatenate([first, (weights - first.astype(np.float32)).astype(ml_dtypes.bfloat16)], axis=1)
 
 
 def beyond_weights():
     row = lax.broadcasted_iota(jnp.int32, (16, LANES), 0)
     lane = lax.broadcasted_iota(jnp.int32, (16, LANES), 1)
     weights = jnp.zeros((16, LANES), jnp.float32)
-    for side, taps in ((0, enumerate(G[15:21])), (8, enumerate(G[0:5], LANES - 5))):
+    for side, taps in ((0, enumerate(EAST[15:21])), (8, enumerate(EAST[:5], LANES - 5))):
         for at, tap in taps:
-            weights = jnp.where((row == side) & (lane == at), tap, weights)
+            weights = jnp.where((row == side) & (lane == at), float(tap), weights)
     return weights
 
 
@@ -193,15 +202,21 @@
     return jnp.dot(a, b, preferred_element_type=jnp.float32)
 
 
-def east_sums(values, pair, weights, third):
+def east_sums(values, pair, weights):
     rows = pl.ds(pair * 2 * LANES, 2 * LANES)
     a, b, c = split_here(values)
     both = dot(a, weights[rows, :]) + dot(b, weights[rows, :])
-    small = dot(a, third[rows, :]) + dot(c, weights[rows, :LANES])
-    return both[:, :LANES] + (both[:, LANES:] + small)
-
-
-def middle_kernel(order, fields, ready, weights, third, inner, partial, later, tile, edge, sems):
+    return both[:, :LANES] + (both[:, LANES:] + dot(c, weights[rows, :LANES]))
+
+
+def east_sums_stacked(values, pair, weights):
+    parts = dot(jnp.concatenate(split_here(values), axis=0), weights[pl.ds(pair * 2 * LANES, 2 * LANES), :])
+    count = values.shape[0]
+    sums = parts[:count] + (parts[count : 2 * count] + parts[2 * count :])
+    return sums[:, :LANES] + sums[:, LANES:]
+
+
+def middle_kernel(order, fields, ready, weights, inner, partial, later, tile, edge, sems):
     places = [tile.at[i] for i in range(FULL - BROUGHT)] + [later.at[i] for i in range(len(order) - FULL)]
     copies = tile_copies(fields, list(zip(order[BROUGHT:], places)), sems)
     for copy in copies:
@@ -210,7 +225,7 @@
 
     def add(pair):
         both = jnp.concatenate([edge[2 * pair], edge[2 * pair + 1]], axis=1)
-        part = east_sums(both, pair, weights, third)
+        part = east_sums(both, pair, weights)
         partial[...] = part if pair == 0 else partial[...] + part
 
     for i in range(len(order)):
@@ -242,7 +257,7 @@
         after[rows, :] = total[q * ROWS + LEVELS : (q + 1) * ROWS]
 
 
-def coarse_kernel(full_inner, later, weights, third, across, beside, coarse, inner):
+def coarse_kernel(full_inner, later, weights, across, beside, coarse, inner):
     count = later.shape[0]
     tiles = [full_inner.at[i] for i in range(FULL)] + [inner.at[i] for i in range(count)]
     stop = TERMS * LEVELS * ROWS
@@ -250,7 +265,7 @@
 
     def add(pair):
         both = jnp.concatenate([tiles[2 * pair][...], tiles[2 * pair + 1][...]], axis=1)
-        coarse[...] += east_sums(both, pair, weights, third)
+        coarse[...] += east_sums(both, pair, weights)
 
     done = 0
     for i in range(count):
@@ -343,7 +358,7 @@
     flat = fields.reshape(COMPONENTS, LEVELS * height, width)
     lane_tile = (COMPONENTS, LEVELS * height, LANES)
     order = (0, tiles - 1) + tuple(range(1, tiles - 1))
-    weights, third = [jnp.asarray(w) for w in split_weights(width, order)]
+    weights = jnp.asarray(split_weights(width, order))
     rest = tiles - FULL
     message = f32(1, rows + 2 * EDGE)
     to_across, to_beside, ready = call(
@@ -371,7 +386,6 @@
         flat,
         ready,
         weights,
-        third,
         scratch=[
             pltpu.VMEM((FULL - BROUGHT, *lane_tile), jnp.float32),
             pltpu.VMEM((tiles, 2 * EDGE, LANES), jnp.float32),
@@ -388,7 +402,6 @@
         full_inner,
         later,
         weights,
-        third,
         across,
         beside,
         scratch=[pltpu.VMEM((rest, rows, LANES), jnp.float32)],

time: 31.7 us -> 31.7 us (level)
  no operation moved by 1% of the time
where the time goes in v6:
time: 31.7 us; the launch traced here: 31.5 us
  blocking collectives  15 us (47%)
  Pallas kernels  9.51 us (30%)
  starting transfers between devices  6.9 us (22%)
    all_to_all x1, blocking collectives, per_device(): lax.all_to_all(outgoing, ('gx', 'gy'), split_axis=0, concat_axis=0, tiled...  15 us
    pallas_call x6, Pallas kernels, call(): pl.pallas_call(kernel, out_shape=out_shape, in_specs=[pl.BlockSpec(memory...  9.51 us
    ppermute x1, starting transfers between devices, per_device(): across = lax.ppermute(to_across, 'gx', across_x)  2.67 us
    ppermute x1, starting transfers between devices, per_device(): from_north = lax.ppermute(before, 'gy', down_y)  2.09 us
    ppermute x1, starting transfers between devices, per_device(): from_south = lax.ppermute(after, 'gy', up_y)  1.35 us
    ppermute x1, starting transfers between devices, per_device(): beside = lax.ppermute(to_beside, 'gx', beside_x)  0.79 us
  transfers between devices with their start and end apart: 4, of which 0 were waited for; matrix products, arithmetic and copies ran while one was open for 0% of the time, Pallas kernels for 19%

profile of v6, /device:TPU:1, one launch (start us, length us, event | category | flops | bytes accessed | tf_op | source)
XLA Modules:
  0.0 31.5 jit_solution(12417024982389715278)
XLA Ops:
  0.0 0.0 copy-start
  0.0 2.0 %shard_map.37 = (f32[1,560]{1,0:T(1,128)S(1)}, f32[1,560]{1,0:T(1,128)S(1)}, f32[4,4,320,128]{3,2,1,0:T(8,128)S(1)}) custom-call(f32[4,320,1280]{2,1,0:T(8,128)} %bitcast.3), custom_call_target="tpu_custom_call" | custom-call | tf_op jit(solution)/shard_map/pallas_call | solution.py:340
  2.0 2.7 %collective-permute-start = (f32[1,560]{1,0:T(1,128)S(1)}, f32[1,560]{1,0:T(1,128)S(1)}, u32[]{:S(2)}, u32[]{:S(2)}) collective-permute-start(f32[1,560]{1,0:T(1,128)S(1)} %get-tuple-element.16), channel_id=1, source_target_pairs={{0,28},{4,8},{8,4},{12,16},{16,12},{20,24},{24,20},{28,0},{1,29},{... | collective-permute-start | bytes 6728 | tf_op jit(solution)/shard_map/ppermute | solution.py:381
  4.7 0.8 %collective-permute-start.1 = (f32[1,560]{1,0:T(1,128)S(1)}, f32[1,560]{1,0:T(1,128)S(1)}, u32[]{:S(2)}, u32[]{:S(2)}) collective-permute-start(f32[1,560]{1,0:T(1,128)S(1)} %get-tuple-element.17), channel_id=1, source_target_pairs={{0,4},{4,0},{8,12},{12,8},{16,20},{20,16},{24,28},{28,24},{1,5},{5... | collective-permute-start | bytes 6728 | tf_op jit(solution)/shard_map/ppermute | solution.py:382
  5.4 0.0 copy-done
  5.5 2.6 %shard_map.38 = (f32[5,448,128]{2,1,0:T(8,128)S(1)}, f32[112,128]{1,0:T(8,128)S(1)}, f32[5,4,320,128]{3,2,1,0:T(8,128)S(1)}) custom-call(f32[4,320,1280]{2,1,0:T(8,128)} %bitcast.4, f32[4,4,320,128]{3,2,1,0:T(8,128)S(1)} %get-tuple-element.13.ready, bf16[1280,256]{1,0:T(8,128)(2,1)S(1)} %copy-done), custom_call_target="tpu_custom_call" | custom-call | tf_op jit(solution)/shard_map/pallas_call | solution.py:340
  8.1 0.0 copy-start.1
  8.1 0.0 collective-permute-done.across
  8.1 0.0 collective-permute-done.1.beside
  8.1 0.3 %shard_map.40 = (f32[56,128]{1,0:T(8,128)S(1)}, f32[56,128]{1,0:T(8,128)S(1)}) custom-call(f32[112,128]{1,0:T(8,128)S(1)} %get-tuple-element.18.partial, f32[1,560]{1,0:T(1,128)S(1)} %collective-permute-done.across, f32[1,560]{1,0:T(1,128)S(1)} %collective-permute-done.1.beside), custom_call_target="tpu_custom_call" | custom-call | tf_op jit(solution)/shard_map/pallas_call | solution.py:340
  8.5 1.4 %collective-permute-start.2 = (f32[56,128]{1,0:T(8,128)S(1)}, f32[56,128]{1,0:T(8,128)S(1)}, u32[]{:S(2)}, u32[]{:S(2)}) collective-permute-start(f32[56,128]{1,0:T(8,128)S(1)} %get-tuple-element.19.after), channel_id=1, source_target_pairs={{0,1},{1,2},{2,3},{3,0},{4,5},{5,6},{6,7},{7,4},{8,9},{9,10},{10,1... | collective-permute-start | bytes 86024 | tf_op jit(solution)/shard_map/ppermute | solution.py:397
  9.8 2.1 %collective-permute-start.3 = (f32[56,128]{1,0:T(8,128)S(1)}, f32[56,128]{1,0:T(8,128)S(1)}, u32[]{:S(2)}, u32[]{:S(2)}) collective-permute-start(f32[56,128]{1,0:T(8,128)S(1)} %get-tuple-element.20.before), channel_id=1, source_target_pairs={{1,0},{2,1},{3,2},{0,3},{5,4},{6,5},{7,6},{4,7},{9,8},{10,9},{11,1... | collective-permute-start | bytes 86024 | tf_op jit(solution)/shard_map/ppermute | solution.py:398
  11.9 3.2 %shard_map.39.coarse = f32[448,128]{1,0:T(8,128)S(1)} custom-call(f32[5,448,128]{2,1,0:T(8,128)S(1)} %get-tuple-element.14.full_inner, f32[5,4,320,128]{3,2,1,0:T(8,128)S(1)} %get-tuple-element.15.later, bf16[1280,256]{1,0:T(8,128)(2,1)S(1)} %copy-done, f32[1,560]{1,0:T(1,128)S(1)} %collective-permute-done.across, f32[1,560]{1,0:T(1,128)S(1)} %collective-permute-done.1.beside), custom_call_target="tpu_custom_call" | custom-call | tf_op jit(solution)/shard_map/pallas_call | solution.py:340
  15.1 0.0 collective-permute-done.2.south
  15.1 0.0 collective-permute-done.3.north
  15.2 0.0 copy-done.1
  15.2 0.6 %shard_map.41 = f32[32,4,640]{2,1,0:T(4,128)S(1)} custom-call(f32[448,128]{1,0:T(8,128)S(1)} %shard_map.39.coarse, f32[56,128]{1,0:T(8,128)S(1)} %collective-permute-done.2.south, f32[56,128]{1,0:T(8,128)S(1)} %collective-permute-done.3.north, f32[56,128]{1,0:T(8,128)S(1)} %get-tuple-element.20.before, f32[56,128]{1,0:T(8,128)S(1)} %get-tuple-element.19.after, ...), custom_call_target="tpu_custom_call" | custom-call | tf_op jit(solution)/shard_map/pallas_call | solution.py:340
  15.8 15.0 %all_to_all.5.arrived = f32[32,4,640]{2,1,0:T(4,128)S(1)} all-to-all(f32[32,4,640]{2,1,0:T(4,128)S(1)} %shard_map.41), channel_id=1, replica_groups=mesh['gx'=8,'gy'=4] {'gx','gy'}, dimensions={0} | all-to-all | bytes 655360 | tf_op jit(solution)/shard_map/all_to_all | solution.py:424
  30.7 0.8 %shard_map.42 = f32[128,640]{1,0:T(8,128)} custom-call(f32[32,4,640]{2,1,0:T(4,128)S(1)} %all_to_all.5.arrived), custom_call_target="tpu_custom_call" | custom-call | tf_op jit(solution)/shard_map/pallas_call | solution.py:340
Async XLA Ops:
  0.0 5.4 %copy-start = (bf16[1280,256]{1,0:T(8,128)(2,1)S(1)}, bf16[1280,256]{1,0:T(8,128)(2,1)}, u32[]{:S(2)}) copy-start(bf16[1280,256]{1,0:T(8,128)(2,1)} %constant.2.clone.weights) | copy-start | bytes 1966084
  2.0 6.1 %collective-permute-start = (f32[1,560]{1,0:T(1,128)S(1)}, f32[1,560]{1,0:T(1,128)S(1)}, u32[]{:S(2)}, u32[]{:S(2)}) collective-permute-start(f32[1,560]{1,0:T(1,128)S(1)} %get-tuple-element.16), channel_id=1, source_target_pairs={{0,28},{4,8},{8,4},{12,16},{16,12},{20,24},{24,20},{28,0},{1,29},{... | collective-permute-start | bytes 6728 | tf_op jit(solution)/shard_map/ppermute | solution.py:381
  4.7 3.5 %collective-permute-start.1 = (f32[1,560]{1,0:T(1,128)S(1)}, f32[1,560]{1,0:T(1,128)S(1)}, u32[]{:S(2)}, u32[]{:S(2)}) collective-permute-start(f32[1,560]{1,0:T(1,128)S(1)} %get-tuple-element.17), channel_id=1, source_target_pairs={{0,4},{4,0},{8,12},{12,8},{16,20},{20,16},{24,28},{28,24},{1,5},{5... | collective-permute-start | bytes 6728 | tf_op jit(solution)/shard_map/ppermute | solution.py:382
  8.1 7.1 %copy-start.1 = (s32[64,1]{0,1:T(1,128)S(1)}, s32[64,1]{0,1:T(1,128)}, u32[]{:S(2)}) copy-start(s32[64,1]{0,1:T(1,128)} %param.4) | copy-start | bytes 772
  8.5 6.7 %collective-permute-start.2 = (f32[56,128]{1,0:T(8,128)S(1)}, f32[56,128]{1,0:T(8,128)S(1)}, u32[]{:S(2)}, u32[]{:S(2)}) collective-permute-start(f32[56,128]{1,0:T(8,128)S(1)} %get-tuple-element.19.after), channel_id=1, source_target_pairs={{0,1},{1,2},{2,3},{3,0},{4,5},{5,6},{6,7},{7,4},{8,9},{9,10},{10,1... | collective-permute-start | bytes 86024 | tf_op jit(solution)/shard_map/ppermute | solution.py:397
  9.8 5.3 %collective-permute-start.3 = (f32[56,128]{1,0:T(8,128)S(1)}, f32[56,128]{1,0:T(8,128)S(1)}, u32[]{:S(2)}, u32[]{:S(2)}) collective-permute-start(f32[56,128]{1,0:T(8,128)S(1)} %get-tuple-element.20.before), channel_id=1, source_target_pairs={{1,0},{2,1},{3,2},{0,3},{5,4},{6,5},{7,6},{4,7},{9,8},{10,9},{11,1... | collective-permute-start | bytes 86024 | tf_op jit(solution)/shard_map/ppermute | solution.py:398

commit v7 on v6

--- a/solution.py
+++ b/solution.py
@@ -225,7 +225,7 @@
 
     def add(pair):
         both = jnp.concatenate([edge[2 * pair], edge[2 * pair + 1]], axis=1)
-        part = east_sums(both, pair, weights)
+        part = east_sums_stacked(both, pair, weights)
         partial[...] = part if pair == 0 else partial[...] + part
 
     for i in range(len(order)):

time: 31.7 us -> 31.6 us (level)
  no operation moved by 1% of the time
where the time goes in v7:
time: 31.6 us; the launch traced here: 31.5 us
  blocking collectives  15 us (47%)
  Pallas kernels  9.49 us (30%)
  starting transfers between devices  6.9 us (22%)
    all_to_all x1, blocking collectives, per_device(): lax.all_to_all(outgoing, ('gx', 'gy'), split_axis=0, concat_axis=0, tiled...  15 us
    pallas_call x6, Pallas kernels, call(): pl.pallas_call(kernel, out_shape=out_shape, in_specs=[pl.BlockSpec(memory...  9.49 us
    ppermute x1, starting transfers between devices, per_device(): across = lax.ppermute(to_across, 'gx', across_x)  2.67 us
    ppermute x1, starting transfers between devices, per_device(): from_north = lax.ppermute(before, 'gy', down_y)  2.09 us
    ppermute x1, starting transfers between devices, per_device(): from_south = lax.ppermute(after, 'gy', up_y)  1.35 us
    ppermute x1, starting transfers between devices, per_device(): beside = lax.ppermute(to_beside, 'gx', beside_x)  0.79 us
  transfers between devices with their start and end apart: 4, of which 0 were waited for; matrix products, arithmetic and copies ran while one was open for 0% of the time, Pallas kernels for 19%

profile of v7, /device:TPU:1, one launch (start us, length us, event | category | flops | bytes accessed | tf_op | source)
XLA Modules:
  0.0 31.5 jit_solution(16582961721716254901)
XLA Ops:
  0.0 0.0 copy-start
  0.0 2.0 %shard_map.37 = (f32[1,560]{1,0:T(1,128)S(1)}, f32[1,560]{1,0:T(1,128)S(1)}, f32[4,4,320,128]{3,2,1,0:T(8,128)S(1)}) custom-call(f32[4,320,1280]{2,1,0:T(8,128)} %bitcast.3), custom_call_target="tpu_custom_call" | custom-call | tf_op jit(solution)/shard_map/pallas_call | solution.py:340
  2.0 2.7 %collective-permute-start = (f32[1,560]{1,0:T(1,128)S(1)}, f32[1,560]{1,0:T(1,128)S(1)}, u32[]{:S(2)}, u32[]{:S(2)}) collective-permute-start(f32[1,560]{1,0:T(1,128)S(1)} %get-tuple-element.16), channel_id=1, source_target_pairs={{0,28},{4,8},{8,4},{12,16},{16,12},{20,24},{24,20},{28,0},{1,29},{... | collective-permute-start | bytes 6728 | tf_op jit(solution)/shard_map/ppermute | solution.py:381
  4.7 0.8 %collective-permute-start.1 = (f32[1,560]{1,0:T(1,128)S(1)}, f32[1,560]{1,0:T(1,128)S(1)}, u32[]{:S(2)}, u32[]{:S(2)}) collective-permute-start(f32[1,560]{1,0:T(1,128)S(1)} %get-tuple-element.17), channel_id=1, source_target_pairs={{0,4},{4,0},{8,12},{12,8},{16,20},{20,16},{24,28},{28,24},{1,5},{5... | collective-permute-start | bytes 6728 | tf_op jit(solution)/shard_map/ppermute | solution.py:382
  5.4 0.0 copy-done
  5.5 2.6 %shard_map.38 = (f32[5,448,128]{2,1,0:T(8,128)S(1)}, f32[112,128]{1,0:T(8,128)S(1)}, f32[5,4,320,128]{3,2,1,0:T(8,128)S(1)}) custom-call(f32[4,320,1280]{2,1,0:T(8,128)} %bitcast.4, f32[4,4,320,128]{3,2,1,0:T(8,128)S(1)} %get-tuple-element.13.ready, bf16[1280,256]{1,0:T(8,128)(2,1)S(1)} %copy-done), custom_call_target="tpu_custom_call" | custom-call | tf_op jit(solution)/shard_map/pallas_call | solution.py:340
  8.1 0.0 copy-start.1
  8.1 0.0 collective-permute-done.across
  8.1 0.0 collective-permute-done.1.beside
  8.1 0.3 %shard_map.40 = (f32[56,128]{1,0:T(8,128)S(1)}, f32[56,128]{1,0:T(8,128)S(1)}) custom-call(f32[112,128]{1,0:T(8,128)S(1)} %get-tuple-element.18.partial, f32[1,560]{1,0:T(1,128)S(1)} %collective-permute-done.across, f32[1,560]{1,0:T(1,128)S(1)} %collective-permute-done.1.beside), custom_call_target="tpu_custom_call" | custom-call | tf_op jit(solution)/shard_map/pallas_call | solution.py:340
  8.4 1.3 %collective-permute-start.2 = (f32[56,128]{1,0:T(8,128)S(1)}, f32[56,128]{1,0:T(8,128)S(1)}, u32[]{:S(2)}, u32[]{:S(2)}) collective-permute-start(f32[56,128]{1,0:T(8,128)S(1)} %get-tuple-element.19.after), channel_id=1, source_target_pairs={{0,1},{1,2},{2,3},{3,0},{4,5},{5,6},{6,7},{7,4},{8,9},{9,10},{10,1... | collective-permute-start | bytes 86024 | tf_op jit(solution)/shard_map/ppermute | solution.py:397
  9.8 2.1 %collective-permute-start.3 = (f32[56,128]{1,0:T(8,128)S(1)}, f32[56,128]{1,0:T(8,128)S(1)}, u32[]{:S(2)}, u32[]{:S(2)}) collective-permute-start(f32[56,128]{1,0:T(8,128)S(1)} %get-tuple-element.20.before), channel_id=1, source_target_pairs={{1,0},{2,1},{3,2},{0,3},{5,4},{6,5},{7,6},{4,7},{9,8},{10,9},{11,1... | collective-permute-start | bytes 86024 | tf_op jit(solution)/shard_map/ppermute | solution.py:398
  11.9 3.2 %shard_map.39.coarse = f32[448,128]{1,0:T(8,128)S(1)} custom-call(f32[5,448,128]{2,1,0:T(8,128)S(1)} %get-tuple-element.14.full_inner, f32[5,4,320,128]{3,2,1,0:T(8,128)S(1)} %get-tuple-element.15.later, bf16[1280,256]{1,0:T(8,128)(2,1)S(1)} %copy-done, f32[1,560]{1,0:T(1,128)S(1)} %collective-permute-done.across, f32[1,560]{1,0:T(1,128)S(1)} %collective-permute-done.1.beside), custom_call_target="tpu_custom_call" | custom-call | tf_op jit(solution)/shard_map/pallas_call | solution.py:340
  15.1 0.0 collective-permute-done.2.south
  15.1 0.0 collective-permute-done.3.north
  15.1 0.0 copy-done.1
  15.1 0.6 %shard_map.41 = f32[32,4,640]{2,1,0:T(4,128)S(1)} custom-call(f32[448,128]{1,0:T(8,128)S(1)} %shard_map.39.coarse, f32[56,128]{1,0:T(8,128)S(1)} %collective-permute-done.2.south, f32[56,128]{1,0:T(8,128)S(1)} %collective-permute-done.3.north, f32[56,128]{1,0:T(8,128)S(1)} %get-tuple-element.20.before, f32[56,128]{1,0:T(8,128)S(1)} %get-tuple-element.19.after, ...), custom_call_target="tpu_custom_call" | custom-call | tf_op jit(solution)/shard_map/pallas_call | solution.py:340
  15.7 15.0 %all_to_all.5.arrived = f32[32,4,640]{2,1,0:T(4,128)S(1)} all-to-all(f32[32,4,640]{2,1,0:T(4,128)S(1)} %shard_map.41), channel_id=1, replica_groups=mesh['gx'=8,'gy'=4] {'gx','gy'}, dimensions={0} | all-to-all | bytes 655360 | tf_op jit(solution)/shard_map/all_to_all | solution.py:424
  30.7 0.8 %shard_map.42 = f32[128,640]{1,0:T(8,128)} custom-call(f32[32,4,640]{2,1,0:T(4,128)S(1)} %all_to_all.5.arrived), custom_call_target="tpu_custom_call" | custom-call | tf_op jit(solution)/shard_map/pallas_call | solution.py:340
Async XLA Ops:
  0.0 5.4 %copy-start = (bf16[1280,256]{1,0:T(8,128)(2,1)S(1)}, bf16[1280,256]{1,0:T(8,128)(2,1)}, u32[]{:S(2)}) copy-start(bf16[1280,256]{1,0:T(8,128)(2,1)} %constant.2.clone.weights) | copy-start | bytes 1966084
  2.0 6.1 %collective-permute-start = (f32[1,560]{1,0:T(1,128)S(1)}, f32[1,560]{1,0:T(1,128)S(1)}, u32[]{:S(2)}, u32[]{:S(2)}) collective-permute-start(f32[1,560]{1,0:T(1,128)S(1)} %get-tuple-element.16), channel_id=1, source_target_pairs={{0,28},{4,8},{8,4},{12,16},{16,12},{20,24},{24,20},{28,0},{1,29},{... | collective-permute-start | bytes 6728 | tf_op jit(solution)/shard_map/ppermute | solution.py:381
  4.7 3.4 %collective-permute-start.1 = (f32[1,560]{1,0:T(1,128)S(1)}, f32[1,560]{1,0:T(1,128)S(1)}, u32[]{:S(2)}, u32[]{:S(2)}) collective-permute-start(f32[1,560]{1,0:T(1,128)S(1)} %get-tuple-element.17), channel_id=1, source_target_pairs={{0,4},{4,0},{8,12},{12,8},{16,20},{20,16},{24,28},{28,24},{1,5},{5... | collective-permute-start | bytes 6728 | tf_op jit(solution)/shard_map/ppermute | solution.py:382
  8.1 7.1 %copy-start.1 = (s32[64,1]{0,1:T(1,128)S(1)}, s32[64,1]{0,1:T(1,128)}, u32[]{:S(2)}) copy-start(s32[64,1]{0,1:T(1,128)} %param.4) | copy-start | bytes 772
  8.4 6.7 %collective-permute-start.2 = (f32[56,128]{1,0:T(8,128)S(1)}, f32[56,128]{1,0:T(8,128)S(1)}, u32[]{:S(2)}, u32[]{:S(2)}) collective-permute-start(f32[56,128]{1,0:T(8,128)S(1)} %get-tuple-element.19.after), channel_id=1, source_target_pairs={{0,1},{1,2},{2,3},{3,0},{4,5},{5,6},{6,7},{7,4},{8,9},{9,10},{10,1... | collective-permute-start | bytes 86024 | tf_op jit(solution)/shard_map/ppermute | solution.py:397
  9.8 5.4 %collective-permute-start.3 = (f32[56,128]{1,0:T(8,128)S(1)}, f32[56,128]{1,0:T(8,128)S(1)}, u32[]{:S(2)}, u32[]{:S(2)}) collective-permute-start(f32[56,128]{1,0:T(8,128)S(1)} %get-tuple-element.20.before), channel_id=1, source_target_pairs={{1,0},{2,1},{3,2},{0,3},{5,4},{6,5},{7,6},{4,7},{9,8},{10,9},{11,1... | collective-permute-start | bytes 86024 | tf_op jit(solution)/shard_map/ppermute | solution.py:398
